TPU v7x, 512 devices: a whole 4x8x8 slice. The times are simulated.
512 devices in a mesh: group: 64 (over z_lo, y, core), tp: 8 (over x, z_hi).
Axes of the slice: x: 4, y: 8, z: 8 (z_hi: 2, z_lo: 4; z = z_hi * 4 + z_lo), core: 2. Of those that a mesh axis runs over, the one named last changes fastest.
Arguments:
- hidden: bfloat16 [3, 512, 5120], P(None, 'group'), may hold values from -6 to 6
- queries: bfloat16 [3, 512, 8192], P(None, 'group', 'tp'), as said below
- key_cache: bfloat16 [512, 512, 1024], P('group', None, 'tp'), as said below
- value_cache: bfloat16 [512, 512, 1024], P('group', None, 'tp'), may hold values from -6 to 6
- lengths: int32 [512], P('group'), may hold values from 1 to 512, 104857 in all
- key_gain: float32 [128], replicated, may hold values from 0.25 to 1.75
- base_weight: bfloat16 [5120, 2048], P(None, 'tp'), may hold values from -0.078125 to 0.078125
- delta_codes: bfloat16 [5120, 2048], P(('group', 'tp')), may hold values from -4 to 4
- delta_scales: bfloat16 [5120, 16], P(('group', 'tp')), may hold values from 0.0049743652 to 0.049804688
Outputs:
- attended: bfloat16 [3, 512, 8192], P(None, 'group', 'tp')
Inputs may be any that keep to these rules, and one draw needn't show every extreme that they name: `queries`: query entries stay within -180 to 180. `key_cache`: cached key entries stay within -6 to 6. `lengths`: some row fills all 512 slots.
All inputs are finite; a program needn't handle non-finite values. No bound on the sum of `lengths` on one device may be relied on, other than what follows from the above.
Results may differ from a plain program's by a relative error of at most 0.0058.
Values may be sent and summed in bfloat16 or wider, within the bound.
A program may use at most 64 MiB of HBM per device.

v0:
```python
import math

import jax
import jax.numpy as jnp
from jax import lax
from jax.sharding import PartitionSpec as P


def rotate_keys(keys, positions):
    half = keys.shape[-1] // 2
    ladder = jnp.arange(half).astype(jnp.float32)
    freqs = jnp.exp(-math.log(1000000.0) * ladder / half)
    angles = positions[..., None] * freqs
    cosine = jnp.cos(angles)
    sine = jnp.sin(angles)
    first = keys[..., :half]
    second = keys[..., half:]
    return jnp.concatenate(
        [first * cosine - second * sine, second * cosine + first * sine], axis=-1
    )


def make_new(projected, key_gain, lengths, steps):
    width = key_gain.shape[0]
    split = projected.reshape(steps, lengths.shape[0], -1, 2, width)
    keys = split[:, :, :, 0, :]
    values = split[:, :, :, 1, :]
    meansq = jnp.mean(keys * keys, axis=-1, keepdims=True)
    keys = keys * lax.rsqrt(meansq + 1e-06) * key_gain
    positions = (lengths[None, :] + jnp.arange(steps)[:, None]).astype(jnp.float32)
    keys = rotate_keys(keys, positions[:, :, None])
    return (keys.astype(jnp.bfloat16), values.astype(jnp.bfloat16))


def attend(queries, key_cache, value_cache, lengths, fresh_keys, fresh_values):
    steps, rowcount, _ = queries.shape
    heads, width = (fresh_keys.shape[2], fresh_keys.shape[3])
    scale = 1.0 / math.sqrt(width)
    queried = queries.reshape(steps, rowcount, heads, -1, width)
    keyset = key_cache.reshape(rowcount, -1, heads, width)
    valset = value_cache.reshape(rowcount, -1, heads, width)
    slots = keyset.shape[1]
    cache_scores = (
        jnp.einsum("srkgd,rckd->srkgc", queried, keyset, preferred_element_type=jnp.float32) * scale
    )
    valid = jnp.arange(slots)[None, :] < lengths[:, None]
    cache_scores = jnp.where(valid[None, :, None, None, :], cache_scores, -1e30)
    fresh_scores = (
        jnp.einsum("srkgd,trkd->srkgt", queried, fresh_keys, preferred_element_type=jnp.float32)
        * scale
    )
    later = jnp.arange(steps)[None, :] <= jnp.arange(steps)[:, None]
    fresh_scores = jnp.where(later[:, None, None, None, :], fresh_scores, -1e30)
    highest = jnp.maximum(jnp.max(cache_scores, axis=-1), jnp.max(fresh_scores, axis=-1))[..., None]
    cache_exp = jnp.exp(cache_scores - highest)
    fresh_exp = jnp.exp(fresh_scores - highest)
    summed = jnp.sum(cache_exp, axis=-1, keepdims=True) + jnp.sum(fresh_exp, axis=-1, keepdims=True)
    cache_probs = (cache_exp / summed).astype(jnp.bfloat16)
    fresh_probs = (fresh_exp / summed).astype(jnp.bfloat16)
    result = jnp.einsum(
        "srkgc,rckd->srkgd", cache_probs, valset, preferred_element_type=jnp.float32
    )
    result = result + jnp.einsum(
        "srkgt,trkd->srkgd", fresh_probs, fresh_values, preferred_element_type=jnp.float32
    )
    return result.reshape(steps, rowcount, -1).astype(jnp.bfloat16)


def dequantize(base_rows, code_rows, scale_rows, width):
    factor = jnp.repeat(scale_rows.astype(jnp.float32), width, axis=1)
    return (base_rows.astype(jnp.float32) + code_rows.astype(jnp.float32) * factor).astype(
        jnp.bfloat16
    )


def per_device(
    hidden,
    queries,
    key_cache,
    value_cache,
    lengths,
    key_gain,
    base_weight,
    delta_codes,
    delta_scales,
):
    width = key_gain.shape[0]
    steps = hidden.shape[0]
    flattened = hidden.reshape(-1, hidden.shape[2])
    gathered_codes, gathered_scales = (
        lax.all_gather(delta_codes, "group", axis=0, tiled=True),
        lax.all_gather(delta_scales, "group", axis=0, tiled=True),
    )
    sorted_codes, sorted_scales = (
        lax.all_to_all(gathered_codes, "tp", split_axis=1, concat_axis=0, tiled=True),
        lax.all_to_all(gathered_scales, "tp", split_axis=1, concat_axis=0, tiled=True),
    )
    replicas = lax.axis_size("group")
    ranks = lax.axis_size("tp")
    owned = delta_codes.shape[0]
    sorted_codes = jnp.transpose(
        sorted_codes.reshape(ranks, replicas, owned, -1), (1, 0, 2, 3)
    ).reshape(base_weight.shape[0], -1)
    sorted_scales = jnp.transpose(
        sorted_scales.reshape(ranks, replicas, owned, -1), (1, 0, 2, 3)
    ).reshape(base_weight.shape[0], -1)
    weight = dequantize(base_weight, sorted_codes, sorted_scales, width)
    projected = jnp.dot(flattened, weight, preferred_element_type=jnp.float32)
    fresh_keys, fresh_values = make_new(projected, key_gain, lengths, steps)
    return attend(queries, key_cache, value_cache, lengths, fresh_keys, fresh_values)


def solution(mesh):
    return jax.shard_map(
        per_device,
        mesh=mesh,
        in_specs=(
            P(None, "group", None),
            P(None, "group", "tp"),
            P("group", None, "tp"),
            P("group", None, "tp"),
            P("group"),
            P(),
            P(None, "tp"),
            P(("group", "tp"), None),
            P(("group", "tp"), None),
        ),
        out_specs=P(None, "group", "tp"),
        check_vma=False,
    )
```

profile of v0, /device:TPU:64, one launch (start us, length us, event | category | flops | bytes accessed | tf_op | source)
XLA Modules:
  0.0 254.2 jit_solution(151062877371878424)
XLA Ops:
  6.5 0.0 copy-start
  6.5 0.0 all-gather.4.cloned.1.call-start
  6.5 0.7 all-gather.4.cloned.1.call-update
  7.3 68.3 %all-gather.1 = bf16[64,10,16]{2,1,0:T(8,128)(2,1)S(1)} all-gather(bf16[1,10,16]{2,1,0:T(8,128)(2,1)} %bitcast.100), channel_id=1, replica_groups=mesh['group'=64,'tp'=8] {'group'}, dimensions={0}, use_global_device_ids=true | all-gather | bytes 20800 | tf_op jit(solution)/shard_map/all_gather | solution.py:92
  75.6 0.7 copy.62
  76.3 1.0 all_to_all.22
  77.3 10.1 %all-to-all-start.1 = ((bf16[640,8,2]{0,2,1:T(2,128)(2,1)}), bf16[640,8,2]{0,2,1:T(2,128)(2,1)S(1)}, u32[]{:S(2)}, u32[]{:S(2)}) async-start(bf16[640,8,2]{0,2,1:T(2,128)(2,1)} %all_to_all.22), calls=%async_computation.1 | async-start | bytes 40960 | tf_op jit(solution)/shard_map/all_to_all | solution.py:96
  87.4 45.6 %all-gather.4.cloned.1.call-done = bf16[64,10,2048]{2,1,0:T(8,128)(2,1)} async-done(((bf16[1,10,2048]{2,1,0:T(8,128)(2,1)}), bf16[64,10,2048]{2,1,0:T(8,128)(2,1)}) %all-gather.4.cloned.1.call-update) | async-done | bytes 2621456 | tf_op jit(solution)/shard_map/all_gather | solution.py:91
  133.0 6.5 %all_to_all.20 = bf16[640,8,256]{2,1,0:T(8,128)(2,1)} reshape(bf16[64,10,2048]{2,1,0:T(8,128)(2,1)} %all-gather.4.cloned.1.call-done) | data formatting | bytes 5242880 | tf_op jit(solution)/shard_map/all_to_all | solution.py:95
  139.5 0.0 copy-start.5
  139.5 0.0 copy-start.4
  139.5 3.8 %copy.59 = bf16[640,8,256]{2,0,1:T(8,128)(2,1)} copy(bf16[640,8,256]{2,1,0:T(8,128)(2,1)} %all_to_all.20) | data formatting | bytes 5242880 | tf_op jit(solution)/shard_map/all_to_all | solution.py:95
  143.3 0.0 all-to-all-done.1
  143.3 8.5 %all-to-all-start = ((bf16[640,8,256]{2,0,1:T(8,128)(2,1)}), bf16[640,8,256]{2,0,1:T(8,128)(2,1)}, u32[]{:S(2)}, u32[]{:S(2)}) async-start(bf16[640,8,256]{2,0,1:T(8,128)(2,1)} %copy.59), calls=%async_computation | async-start | bytes 5242880 | tf_op jit(solution)/shard_map/all_to_all | solution.py:95
  151.9 0.0 copy-done.5
  151.9 0.1 iota_compare_fusion
  152.0 0.0 copy-done
  152.0 0.0 copy-done.4
  152.0 0.5 fusion.38
  152.5 0.5 reshape.241
  153.0 0.3 copy.64
  153.3 0.3 reshape.239
  153.7 2.3 copy.65
  155.9 61.0 %all-to-all-done = bf16[640,8,256]{2,0,1:T(8,128)(2,1)} async-done(((bf16[640,8,256]{2,0,1:T(8,128)(2,1)}), bf16[640,8,256]{2,0,1:T(8,128)(2,1)}, u32[]{:S(2)}, u32[]{:S(2)}) %all-to-all-start) | async-done | bytes 2621472 | tf_op jit(solution)/shard_map/all_to_all | solution.py:95
  216.9 3.3 %copy_convert_fusion = f32[640,8,256]{2,1,0:T(8,128)S(1)} fusion(bf16[640,8,256]{2,0,1:T(8,128)(2,1)} %all-to-all-done), kind=kLoop, calls=%fused_computation.3 | loop fusion | flops 1310720 | bytes 7864320 | tf_op jit(solution)/shard_map/convert_element_type | solution.py:71
  220.2 5.7 %copy.61 = f32[64,8,10,256]{3,2,1,0:T(8,128)} copy(f32[64,8,10,256]{3,1,2,0:T(8,128)S(1)} %bitcast.95) | data formatting | bytes 10485760 | tf_op jit(solution)/shard_map/convert_element_type | solution.py:71
  225.9 0.0 copy-start.3
  225.9 8.0 %reshape.238 = f32[5120,256]{1,0:T(8,128)} reshape(f32[64,8,10,256]{3,2,1,0:T(8,128)} %copy.61) | data formatting | bytes 10485760 | tf_op jit(solution)/shard_map/convert_element_type | solution.py:71
  233.9 0.0 copy-start.1
  233.9 0.0 copy-start.2
  233.9 10.5 %broadcast_in_dim.29 = f32[5120,2,128]{2,1,0:T(2,128)S(1)} broadcast(f32[5120,2]{1,0:T(8,128)} %copy.65), dimensions={0,1} | broadcast | bytes 5283840 | tf_op jit(solution)/shard_map/broadcast_in_dim | solution.py:70
  244.4 0.0 copy-done.3
  244.4 0.0 copy-done.1
  244.4 0.0 copy-done.2
  244.4 0.0 copy-start.6
  244.4 0.0 copy-start.7
  244.4 0.7 fusion.10
  245.2 0.1 multiply_reduce_fusion
  245.3 0.0 copy-done.6
  245.3 0.1 multiply_multiply_fusion
  245.3 0.1 fusion.37
  245.5 0.1 maximum_bitcast_fusion
  245.6 0.3 fusion.39
  245.9 0.1 fusion.22
  245.9 0.2 fusion.16
  246.2 0.0 copy-done.7
  246.2 0.3 convolution_bitcast_fusion
  246.5 0.2 fusion.8
  246.7 0.6 convert_element_type.99
  (10 shorter events, 0.1 us)
Async XLA Ops:
  6.5 145.5 %copy-start = (bf16[8,512,128]{2,1,0:T(8,128)(2,1)S(1)}, bf16[8,512,128]{2,1,0:T(8,128)(2,1)}, u32[]{:S(2)}) copy-start(bf16[8,512,128]{2,1,0:T(8,128)(2,1)} %param.11) | copy-start | bytes 3145732
  6.5 126.5 %all-gather.4.cloned.1.call-start = ((), (), s32[]{:S(2)}) async-start(), calls=%async_computation.2 | async-start | bytes 4259840 | tf_op jit(solution)/shard_map/all_gather | solution.py:91
  77.3 66.1 %all-to-all-start.1 = ((bf16[640,8,2]{0,2,1:T(2,128)(2,1)}), bf16[640,8,2]{0,2,1:T(2,128)(2,1)S(1)}, u32[]{:S(2)}, u32[]{:S(2)}) async-start(bf16[640,8,2]{0,2,1:T(2,128)(2,1)} %all_to_all.22), calls=%async_computation.1 | async-start | bytes 40960 | tf_op jit(solution)/shard_map/all_to_all | solution.py:96
  139.5 12.4 %copy-start.5 = (s32[8]{0:T(128)S(1)}, s32[8]{0:T(128)}, u32[]{:S(2)}) copy-start(s32[8]{0:T(128)} %param.13) | copy-start | bytes 100
  139.5 12.5 %copy-start.4 = (bf16[3,8,1024]{2,1,0:T(8,128)(2,1)S(1)}, bf16[3,8,1024]{2,1,0:T(8,128)(2,1)}, u32[]{:S(2)}) copy-start(bf16[3,8,1024]{2,1,0:T(8,128)(2,1)} %param.10) | copy-start | bytes 147460
  143.3 73.6 %all-to-all-start = ((bf16[640,8,256]{2,0,1:T(8,128)(2,1)}), bf16[640,8,256]{2,0,1:T(8,128)(2,1)}, u32[]{:S(2)}, u32[]{:S(2)}) async-start(bf16[640,8,256]{2,0,1:T(8,128)(2,1)} %copy.59), calls=%async_computation | async-start | bytes 5242880 | tf_op jit(solution)/shard_map/all_to_all | solution.py:95
  225.9 18.5 %copy-start.3 = (bf16[3,8,5120]{2,1,0:T(8,128)(2,1)S(1)}, bf16[3,8,5120]{2,1,0:T(8,128)(2,1)}, u32[]{:S(2)}) copy-start(bf16[3,8,5120]{2,1,0:T(8,128)(2,1)} %param.9) | copy-start | bytes 737284
  233.9 10.5 %copy-start.1 = (f32[5120,256]{1,0:T(8,128)S(1)}, f32[5120,256]{1,0:T(8,128)}, u32[]{:S(2)}) copy-start(f32[5120,256]{1,0:T(8,128)} %reshape.238) | copy-start | bytes 15728644
  233.9 10.5 %copy-start.2 = (bf16[5120,256]{1,0:T(8,128)(2,1)S(1)}, bf16[5120,256]{1,0:T(8,128)(2,1)}, u32[]{:S(2)}) copy-start(bf16[5120,256]{1,0:T(8,128)(2,1)} %param.15) | copy-start | bytes 7864324
  244.4 0.9 copy-start.6
  244.4 1.7 copy-start.7
Sparse Core Ops, SparseCore 0:
  9.5 123.4 all-gather.3
where the time goes:
time: 255 us; the launch traced here: 254 us
  waiting for transfers between devices  107 us (42%)
  blocking collectives  68.3 us (27%)
  local copies, waits for them, and re-layouts  40.2 us (16%)
  starting transfers between devices  18.6 us (7%)
  between operations  13.6 us (5%)
  other arithmetic  4.04 us (2%)
    all_gather x1, blocking collectives, per_device(): lax.all_gather(delta_scales, 'group', axis=0, tiled=True)  68.3 us
    all_to_all x1, waiting for transfers between devices, per_device(): lax.all_to_all(gathered_codes, 'tp', split_axis=1, concat_axis=0, tiled=T...  61 us
    all_gather x1, waiting for transfers between devices, per_device(): lax.all_gather(delta_codes, 'group', axis=0, tiled=True)  45.6 us
    convert_element_type x2, local copies, waits for them, and re-layouts, dequantize(): code_rows.astype(jnp.float32) * factor  13.7 us
    broadcast_in_dim x1, local copies, waits for them, and re-layouts, dequantize(): factor = jnp.repeat(scale_rows.astype(jnp.float32), width, axis=1)  10.5 us
    all_to_all x2, local copies, waits for them, and re-layouts, per_device(): lax.all_to_all(gathered_codes, 'tp', split_axis=1, concat_axis=0, tiled=T...  10.3 us
    all_to_all x1, starting transfers between devices, per_device(): lax.all_to_all(gathered_scales, 'tp', split_axis=1, concat_axis=0, tiled=...  10.1 us
    all_to_all x1, starting transfers between devices, per_device(): lax.all_to_all(gathered_codes, 'tp', split_axis=1, concat_axis=0, tiled=T...  8.54 us
  transfers between devices with their start and end apart: 3, of which 2 were waited for; matrix products, arithmetic and copies ran while one was open for 3% of the time, Pallas kernels for 0%

commit v1 on v0

v1 whole, which is shorter than its diff:
```python
import functools
import math

import jax
import jax.numpy as jnp
from jax import lax
from jax.experimental import pallas as pl
from jax.experimental.pallas import tpu as pltpu
from jax.sharding import PartitionSpec as P

MESH = pl.DeviceIdType.MESH
F32 = jnp.float32
BF16 = jnp.bfloat16

STEPS = 3
ROWS = 8
HD = 128
HEADS = 8
CAP = 512
D = 5120
OWNED = 10
CHUNK = 80
WIDE = 256
WINDOW = 384
QROWS = STEPS * HEADS
ALLQ = ROWS * QROWS
FRESH = STEPS * ROWS
EARLY = 4


def iota(shape, dim):
    return lax.broadcasted_iota(jnp.int32, shape, dim)


def dot(a, b):
    return jnp.dot(a, b, preferred_element_type=F32)


def dot_t(a, b):
    return lax.dot_general(a, b, (((1,), (1,)), ((), ())), preferred_element_type=F32)


def swap_matrix():
    shape = (8, STEPS, 8, ALLQ)
    hit = iota(shape, 3) == iota(shape, 2) * QROWS + iota(shape, 1) * 8 + iota(shape, 0)
    return jnp.where(hit, 1.0, 0.0).astype(F32).reshape(ALLQ, ALLQ).astype(BF16)


def kernel(
    lengths_hbm, gain_hbm, codes_hbm, scales_hbm, base_hbm, hidden_hbm, queries_hbm, kc_hbm, vc_hbm,
    out_ref,
    lens, gain, codes, scales, basebuf, qbuf, kc, vc,
    msg, inbox, wbuf, hbuf, pout, pin, qall, acc, mbuf, lbuf, cosb, sinb,
    local_sem, own_sem, s1, r1, sh, rh, s2, r2, s3, r3,
):
    g = lax.axis_index("group")
    t = lax.axis_index("tp")
    ci = lax.rem(lax.div(g, 16), 2) * 4 + lax.rem(g, 4)
    b = lax.div(g, 32) * 4 + lax.rem(lax.div(g, 4), 4)

    def group_of(c, m):
        return lax.div(m, 4) * 32 + lax.div(c, 4) * 16 + lax.rem(m, 4) * 4 + lax.rem(c, 4)

    def window(m, half):
        q = lax.div(m, 4) * 8 + half * 4 + lax.rem(m, 4)
        return pl.ds(pl.multiple_of(q * 320 - lax.rem(m, 2) * 64, 128), WINDOW)

    def other(mine, k):
        return lax.rem(mine + k, 8)

    loads = [
        pltpu.make_async_copy(src, dst, local_sem.at[i])
        for i, (src, dst) in enumerate(
            [
                (codes_hbm, codes),
                (scales_hbm, scales),
                (lengths_hbm, lens),
                (queries_hbm, qbuf),
                (gain_hbm, gain),
                (base_hbm.at[pl.ds(pl.multiple_of(g * CHUNK, 16), CHUNK), :], basebuf),
                (kc_hbm, kc),
                (vc_hbm, vc),
            ]
        )
    ]
    for load in loads:
        load.start()
    own_hidden = [
        pltpu.make_async_copy(hidden_hbm.at[:, :, window(b, half)], hbuf.at[b, half], own_sem.at[half])
        for half in range(2)
    ]
    for copy in own_hidden:
        copy.start()

    wbuf[:, pl.ds(pl.multiple_of(320 * (1 - lax.rem(b, 2)), 64), 64), :] = jnp.zeros((2, 64, WIDE), BF16)

    barrier = pltpu.get_barrier_semaphore()
    for k in range(1, 8):
        pl.semaphore_signal(barrier, inc=1, device_id=(g, other(t, k)), device_id_type=MESH)
    for k in range(1, 8):
        pl.semaphore_signal(barrier, inc=1, device_id=(group_of(ci, other(b, k)), t), device_id_type=MESH)
    for k in range(1, 8):
        pl.semaphore_signal(barrier, inc=1, device_id=(group_of(other(ci, k), b), t), device_id_type=MESH)

    msg[...] = jnp.zeros((8, 16, WIDE + 128), BF16)
    loads[0].wait()
    loads[1].wait()
    for k in range(8):
        msg[k, 0:OWNED, 0:WIDE] = codes[:, k * WIDE : (k + 1) * WIDE]
        msg[k, 0:OWNED, WIDE : WIDE + 16] = scales[...]

    pl.semaphore_wait(barrier, 21)

    def to_rank(k):
        peer = other(t, k)
        return pltpu.make_async_remote_copy(
            msg.at[peer], inbox.at[t], s1.at[k], r1.at[t], device_id=(g, peer), device_id_type=MESH
        )

    def from_rank(k):
        peer = other(t, k)
        return pltpu.make_async_remote_copy(
            msg.at[t], inbox.at[peer], s1.at[k], r1.at[peer], device_id=(g, peer), device_id_type=MESH
        )

    def hidden_out(k, half):
        peer = other(b, k)
        return pltpu.make_async_remote_copy(
            hidden_hbm.at[:, :, window(peer, half)],
            hbuf.at[b, half],
            sh.at[k, half],
            rh.at[b, half],
            device_id=(group_of(ci, peer), t),
            device_id_type=MESH,
        )

    def hidden_in(k, half):
        peer = other(b, k)
        return pltpu.make_async_remote_copy(
            hidden_hbm.at[:, :, window(b, half)],
            hbuf.at[peer, half],
            sh.at[k, half],
            rh.at[peer, half],
            device_id=(group_of(ci, peer), t),
            device_id_type=MESH,
        )

    def place(c):
        return wbuf.at[lax.div(c, 4), pl.ds(pl.multiple_of(64 * lax.rem(b, 2) + CHUNK * lax.rem(c, 4), 16), CHUNK), :]

    def weight_copy(k, owner):
        peer = other(ci, k)
        return pltpu.make_async_remote_copy(
            place(owner), place(owner), s2.at[k], r2.at[owner],
            device_id=(group_of(peer, b), t), device_id_type=MESH,
        )

    def sum_out(k):
        peer = other(b, k)
        return pltpu.make_async_remote_copy(
            pout.at[peer], pin.at[b], s3.at[k], r3.at[b], device_id=(group_of(ci, peer), t), device_id_type=MESH
        )

    def sum_in(k):
        peer = other(b, k)
        return pltpu.make_async_remote_copy(
            pout.at[b], pin.at[peer], s3.at[k], r3.at[peer], device_id=(group_of(ci, peer), t), device_id_type=MESH
        )

    for k in range(1, 8):
        to_rank(k).start()
    for k in range(1, 8):
        for half in range(2):
            hidden_out(k, half).start()
    inbox[t] = msg[t]

    loads[3].wait()
    swap = swap_matrix()
    flat = qbuf[...].astype(F32).reshape(FRESH, HEADS * HD)
    stacked = jnp.concatenate([flat[:, h * HD : (h + 1) * HD] for h in range(HEADS)], axis=0)
    qall[...] = dot(swap, stacked.astype(BF16))

    loads[2].wait()
    lane = iota((ROWS, HD), 1)
    row = iota((ROWS, HD), 0)
    start = jnp.zeros((ROWS, HD), F32)
    for r in range(ROWS):
        start = jnp.where(row == r, lens[r].astype(F32), start)
    ladder = jnp.where(lane < HD // 2, lane, lane - HD // 2).astype(F32)
    freqs = jnp.exp(-math.log(1000000.0) * ladder / (HD // 2))
    for s in range(STEPS):
        angles = (start + float(s)) * freqs
        cosb[s * ROWS : (s + 1) * ROWS, :] = jnp.cos(angles)
        sine = jnp.sin(angles)
        sinb[s * ROWS : (s + 1) * ROWS, :] = jnp.where(lane < HD // 2, -sine, sine)

    loads[6].wait()
    loads[7].wait()
    scale = 1.0 / math.sqrt(HD)

    def attend(r, carry):
        rows = pl.ds(pl.multiple_of(r * QROWS, 8), QROWS)
        scores = dot_t(qall[rows, :].astype(BF16), kc[r]) * scale
        scores = jnp.where(iota((QROWS, CAP), 1) < lens[r], scores, -1e30)
        highest = jnp.max(scores, axis=-1, keepdims=True)
        weights = jnp.exp(scores - highest)
        mbuf[rows, :] = jnp.broadcast_to(highest, (QROWS, HD))
        lbuf[rows, :] = jnp.broadcast_to(jnp.sum(weights, axis=-1, keepdims=True), (QROWS, HD))
        acc[rows, :] = dot(weights.astype(BF16), vc[r])
        return carry

    lax.fori_loop(0, EARLY, attend, 0)

    loads[4].wait()
    loads[5].wait()
    for k in range(1, 8):
        from_rank(k).wait_recv()
    i = iota((CHUNK, 128), 0)
    packed = i + 6 * lax.shift_right_logical(i * 205, 11)
    pick = jnp.where(iota((CHUNK, 128), 1) == packed, 1.0, 0.0).astype(BF16)
    got = dot(pick, inbox[...].reshape(128, WIDE + 128))
    half_of = jnp.where(iota((128, WIDE), 1) >= HD, 1, 0)
    spread = jnp.where(iota((128, WIDE), 0) == 2 * t + half_of, 1.0, 0.0).astype(BF16)
    factor = dot(got[:, WIDE:].astype(BF16), spread)
    place(ci)[...] = (basebuf[...].astype(F32) + got[:, :WIDE] * factor).astype(BF16)
    for k in range(1, 8):
        weight_copy(k, ci).start()

    lax.fori_loop(EARLY, ROWS, attend, 0)

    for copy in own_hidden:
        copy.wait()
    for k in range(1, 8):
        for half in range(2):
            hidden_in(k, half).wait_recv()
    lefts = [hbuf[:, half].astype(F32).reshape(8 * FRESH, WINDOW).astype(BF16) for half in range(2)]
    for k in range(1, 8):
        weight_copy(k, other(ci, k)).wait_recv()
    partial = dot(lefts[0], wbuf[0]) + dot(lefts[1], wbuf[1])
    pout[...] = partial.reshape(8, FRESH, WIDE)
    for k in range(1, 8):
        sum_out(k).start()
    pin[b] = pout[b]
    swap = swap_matrix()
    everything = qall[...].astype(BF16)
    shape = (ROWS, STEPS, HEADS, FRESH)
    col = iota(shape, 3)
    slot = jnp.where(col >= 2 * ROWS, 2, jnp.where(col >= ROWS, 1, 0))
    seen = (col - slot * ROWS == iota(shape, 0)) & (slot <= iota(shape, 1))
    bias = jnp.where(seen, 0.0, -1e30).astype(F32).reshape(ALLQ, FRESH)
    for k in range(1, 8):
        sum_in(k).wait_recv()
    projected = pin[0]
    for m in range(1, 8):
        projected = projected + pin[m]

    keys = projected[:, :HD]
    meansq = jnp.mean(keys * keys, axis=-1, keepdims=True)
    keys = keys * lax.rsqrt(meansq + 1e-06) * gain[...]
    turned = jnp.concatenate([keys[:, HD // 2 :], keys[:, : HD // 2]], axis=1)
    keys = (keys * cosb[...] + turned * sinb[...]).astype(BF16)
    values = projected[:, HD:].astype(BF16)

    scores = dot_t(everything, keys) * scale + bias
    before = mbuf[...]
    highest = jnp.maximum(before[:, :1], jnp.max(scores, axis=-1, keepdims=True))
    weights = jnp.exp(scores - highest)
    shrink = jnp.exp(before - highest)
    total = shrink * lbuf[...] + jnp.sum(weights, axis=-1, keepdims=True)
    result = (shrink * acc[...] + dot(weights.astype(BF16), values)) / total
    result = dot(swap, result.astype(BF16))
    result = jnp.concatenate([result[h * FRESH : (h + 1) * FRESH, :] for h in range(HEADS)], axis=1)
    out_ref[...] = result.reshape(STEPS, ROWS, HEADS * HD).astype(BF16)

    for k in range(1, 8):
        to_rank(k).wait_send()
        for half in range(2):
            hidden_out(k, half).wait_send()
        weight_copy(k, ci).wait_send()
        sum_out(k).wait_send()


def per_device(hidden, queries, key_cache, value_cache, lengths, key_gain, base_weight, delta_codes, delta_scales):
    dma = pltpu.SemaphoreType.DMA
    return pl.pallas_call(
        kernel,
        out_shape=jax.ShapeDtypeStruct((STEPS, ROWS, HEADS * HD), BF16),
        in_specs=[pl.BlockSpec(memory_space=pl.ANY)] * 9,
        out_specs=pl.BlockSpec(memory_space=pltpu.VMEM),
        scratch_shapes=[
            pltpu.SMEM((ROWS,), jnp.int32),
            pltpu.VMEM((1, HD), F32),
            pltpu.VMEM((OWNED, 8 * WIDE), BF16),
            pltpu.VMEM((OWNED, 16), BF16),
            pltpu.VMEM((CHUNK, WIDE), BF16),
            pltpu.VMEM((STEPS, ROWS, HEADS * HD), BF16),
            pltpu.VMEM((ROWS, CAP, HD), BF16),
            pltpu.VMEM((ROWS, CAP, HD), BF16),
            pltpu.VMEM((8, 16, WIDE + 128), BF16),
            pltpu.VMEM((8, 16, WIDE + 128), BF16),
            pltpu.VMEM((2, WINDOW, WIDE), BF16),
            pltpu.VMEM((8, 2, STEPS, ROWS, WINDOW), BF16),
            pltpu.VMEM((8, FRESH, WIDE), F32),
            pltpu.VMEM((8, FRESH, WIDE), F32),
            pltpu.VMEM((ALLQ, HD), F32),
            pltpu.VMEM((ALLQ, HD), F32),
            pltpu.VMEM((ALLQ, HD), F32),
            pltpu.VMEM((ALLQ, HD), F32),
            pltpu.VMEM((FRESH, HD), F32),
            pltpu.VMEM((FRESH, HD), F32),
            dma((8,)), dma((2,)),
            dma((8,)), dma((8,)),
            dma((8, 2)), dma((8, 2)),
            dma((8,)), dma((8,)),
            dma((8,)), dma((8,)),
        ],
        compiler_params=pltpu.CompilerParams(
            collective_id=0, has_side_effects=True, vmem_limit_bytes=56 * 1024 * 1024
        ),
        name="project_and_attend",
    )(
        lengths, key_gain.reshape(1, HD), delta_codes, delta_scales, base_weight, hidden, queries, key_cache, value_cache,
    )


def solution(mesh):
    return jax.shard_map(
        per_device,
        mesh=mesh,
        in_specs=(
            P(None, "group", None),
            P(None, "group", "tp"),
            P("group", None, "tp"),
            P("group", None, "tp"),
            P("group"),
            P(),
            P(None, "tp"),
            P(("group", "tp"), None),
            P(("group", "tp"), None),
        ),
        out_specs=P(None, "group", "tp"),
        check_vma=False,
    )
```

time: 255 us -> 40.4 us (0.16)
  the two profiles are of different devices: /device:TPU:64 before, /device:TPU:49 now
where the time goes in v1:
time: 40.4 us; the launch traced here: 40.2 us
  Pallas kernels  38.8 us (96%)
  local copies, waits for them, and re-layouts  1.42 us (4%)
    pallas_call x1, Pallas kernels, per_device(): pl.pallas_call(kernel, out_shape=jax.ShapeDtypeStruct((STEPS, ROWS, HEADS...  38.8 us
    unnamed x1, local copies, waits for them, and re-layouts  1.42 us

profile of v1, /device:TPU:49, one launch (start us, length us, event | category | flops | bytes accessed | tf_op | source)
XLA Modules:
  0.0 40.2 jit_solution(17515451308622828034)
XLA Ops:
  0.0 38.8 %project_and_attend.1 = bf16[3,8,1024]{2,1,0:T(8,128)(2,1)} custom-call(s32[8]{0:T(128)} %lengths_hbm.1, f32[1,128]{1,0:T(1,128)} %bitcast.1, bf16[10,2048]{1,0:T(8,128)(2,1)} %codes_hbm.1, bf16[10,16]{1,0:T(8,128)(2,1)} %scales_hbm.1, bf16[5120,256]{1,0:T(8,128)(2,1)} %base_hbm.1, bf16[3,8,5120]{2,1,0:T(8,128)(2,1)} %hidden_hbm.1, ...), custom_call_target="tpu_custom_call" | custom-call | tf_op jit(solution)/shard_map/project_and_attend/pallas_call | solution.py:285
  38.8 1.4 %copy.11 = bf16[3,8,1024]{2,1,0:T(8,128)(2,1)} copy(bf16[3,8,1024]{2,1,0:T(8,128)(2,1)} %project_and_attend.1) | data formatting | bytes 98304

commit v2 on v1

--- a/solution.py
+++ b/solution.py
@@ -50,19 +50,33 @@
     lengths_hbm, gain_hbm, codes_hbm, scales_hbm, base_hbm, hidden_hbm, queries_hbm, kc_hbm, vc_hbm,
     out_ref,
     lens, gain, codes, scales, basebuf, qbuf, kc, vc,
-    msg, inbox, wbuf, hbuf, pout, pin, qall, acc, mbuf, lbuf, cosb, sinb,
-    local_sem, own_sem, s1, r1, sh, rh, s2, r2, s3, r3,
+    msg, inbox, packed, arrived, wbuf, hbuf, pout, pin, qall, acc, mbuf, lbuf, cosb, sinb,
+    local_sem, base_sem, own_sem, s1, r1, sh, rh, s2, r2, sf, rf, s3, r3,
 ):
     g = lax.axis_index("group")
     t = lax.axis_index("tp")
-    ci = lax.rem(lax.div(g, 16), 2) * 4 + lax.rem(g, 4)
-    b = lax.div(g, 32) * 4 + lax.rem(lax.div(g, 4), 4)
-
-    def group_of(c, m):
-        return lax.div(m, 4) * 32 + lax.div(c, 4) * 16 + lax.rem(m, 4) * 4 + lax.rem(c, 4)
+    core = lax.rem(g, 2)
+    y0 = lax.rem(lax.div(g, 2), 2)
+    y1 = lax.rem(lax.div(g, 4), 2)
+    y2 = lax.rem(lax.div(g, 8), 2)
+    z0 = lax.rem(lax.div(g, 16), 2)
+    z1 = lax.div(g, 32)
+    x, zh = lax.div(t, 2), lax.rem(t, 2)
+    b = z1 * 4 + y2 * 2 + y1
+
+    def peer_x(k):
+        return lax.rem(x + k, 4)
+
+    def member(m):
+        return lax.div(m, 4) * 32 + z0 * 16 + lax.rem(m, 4) * 4 + y0 * 2 + core
+
+    def across(j):
+        return (1 - z1) * 32 + (j // 2) * 16 + y2 * 8 + y1 * 4 + (j % 2) * 2 + core
+
+    sibling = g + 1 - 2 * core
 
     def window(m, half):
-        q = lax.div(m, 4) * 8 + half * 4 + lax.rem(m, 4)
+        q = (1 - lax.div(m, 4)) * 8 + half * 4 + lax.rem(m, 4)
         return pl.ds(pl.multiple_of(q * 320 - lax.rem(m, 2) * 64, 128), WINDOW)
 
     def other(mine, k):
@@ -77,102 +91,113 @@
                 (lengths_hbm, lens),
                 (queries_hbm, qbuf),
                 (gain_hbm, gain),
-                (base_hbm.at[pl.ds(pl.multiple_of(g * CHUNK, 16), CHUNK), :], basebuf),
                 (kc_hbm, kc),
                 (vc_hbm, vc),
             ]
         )
     ]
-    for load in loads:
-        load.start()
+    base_loads = [
+        pltpu.make_async_copy(
+            base_hbm.at[pl.ds(pl.multiple_of(across(j) * CHUNK, 16), CHUNK), :], basebuf.at[j], base_sem.at[j]
+        )
+        for j in range(4)
+    ]
     own_hidden = [
         pltpu.make_async_copy(hidden_hbm.at[:, :, window(b, half)], hbuf.at[b, half], own_sem.at[half])
         for half in range(2)
     ]
-    for copy in own_hidden:
-        copy.start()
-
-    wbuf[:, pl.ds(pl.multiple_of(320 * (1 - lax.rem(b, 2)), 64), 64), :] = jnp.zeros((2, 64, WIDE), BF16)
 
     barrier = pltpu.get_barrier_semaphore()
-    for k in range(1, 8):
-        pl.semaphore_signal(barrier, inc=1, device_id=(g, other(t, k)), device_id_type=MESH)
-    for k in range(1, 8):
-        pl.semaphore_signal(barrier, inc=1, device_id=(group_of(ci, other(b, k)), t), device_id_type=MESH)
-    for k in range(1, 8):
-        pl.semaphore_signal(barrier, inc=1, device_id=(group_of(other(ci, k), b), t), device_id_type=MESH)
-
-    msg[...] = jnp.zeros((8, 16, WIDE + 128), BF16)
+    loads[0].start()
+    loads[1].start()
+    for k in range(1, 4):
+        pl.semaphore_signal(barrier, inc=1, device_id=(g, peer_x(k) * 2 + zh), device_id_type=MESH)
+    for j in range(4):
+        for half in range(2):
+            pl.semaphore_signal(barrier, inc=1, device_id=(across(j), x * 2 + half), device_id_type=MESH)
+    for k in range(1, 8):
+        pl.semaphore_signal(barrier, inc=1, device_id=(member(other(b, k)), t), device_id_type=MESH)
+    pl.semaphore_signal(barrier, inc=1, device_id=(sibling, t), device_id_type=MESH)
+    for load in loads[2:]:
+        load.start()
+    for load in own_hidden + base_loads:
+        load.start()
+
+    msg[...] = jnp.zeros(msg.shape, BF16)
     loads[0].wait()
     loads[1].wait()
-    for k in range(8):
-        msg[k, 0:OWNED, 0:WIDE] = codes[:, k * WIDE : (k + 1) * WIDE]
-        msg[k, 0:OWNED, WIDE : WIDE + 16] = scales[...]
-
-    pl.semaphore_wait(barrier, 21)
-
-    def to_rank(k):
-        peer = other(t, k)
-        return pltpu.make_async_remote_copy(
-            msg.at[peer], inbox.at[t], s1.at[k], r1.at[t], device_id=(g, peer), device_id_type=MESH
-        )
-
-    def from_rank(k):
-        peer = other(t, k)
-        return pltpu.make_async_remote_copy(
-            msg.at[t], inbox.at[peer], s1.at[k], r1.at[peer], device_id=(g, peer), device_id_type=MESH
+    for k in range(4):
+        msg[k, 0:OWNED, 0 : 2 * WIDE] = codes[:, k * 2 * WIDE : (k + 1) * 2 * WIDE]
+        msg[k, 0:OWNED, 2 * WIDE : 2 * WIDE + 16] = scales[...]
+
+    def to_x(k):
+        return pltpu.make_async_remote_copy(
+            msg.at[peer_x(k)], inbox.at[x], s1.at[k], r1.at[x],
+            device_id=(g, peer_x(k) * 2 + zh), device_id_type=MESH,
+        )
+
+    def from_x(k):
+        return pltpu.make_async_remote_copy(
+            msg.at[x], inbox.at[peer_x(k)], s1.at[k], r1.at[peer_x(k)],
+            device_id=(g, peer_x(k) * 2 + zh), device_id_type=MESH,
         )
 
     def hidden_out(k, half):
         peer = other(b, k)
         return pltpu.make_async_remote_copy(
-            hidden_hbm.at[:, :, window(peer, half)],
-            hbuf.at[b, half],
-            sh.at[k, half],
-            rh.at[b, half],
-            device_id=(group_of(ci, peer), t),
-            device_id_type=MESH,
+            hidden_hbm.at[:, :, window(peer, half)], hbuf.at[b, half], sh.at[k, half], rh.at[b, half],
+            device_id=(member(peer), t), device_id_type=MESH,
         )
 
     def hidden_in(k, half):
         peer = other(b, k)
         return pltpu.make_async_remote_copy(
-            hidden_hbm.at[:, :, window(b, half)],
-            hbuf.at[peer, half],
-            sh.at[k, half],
-            rh.at[peer, half],
-            device_id=(group_of(ci, peer), t),
-            device_id_type=MESH,
-        )
-
-    def place(c):
-        return wbuf.at[lax.div(c, 4), pl.ds(pl.multiple_of(64 * lax.rem(b, 2) + CHUNK * lax.rem(c, 4), 16), CHUNK), :]
-
-    def weight_copy(k, owner):
-        peer = other(ci, k)
-        return pltpu.make_async_remote_copy(
-            place(owner), place(owner), s2.at[k], r2.at[owner],
-            device_id=(group_of(peer, b), t), device_id_type=MESH,
+            hidden_hbm.at[:, :, window(b, half)], hbuf.at[peer, half], sh.at[k, half], rh.at[peer, half],
+            device_id=(member(peer), t), device_id_type=MESH,
+        )
+
+    def codes_out(j, half):
+        source = (z0 * 2 + y0) * 2 + zh
+        return pltpu.make_async_remote_copy(
+            packed.at[half], arrived.at[source], s2.at[2 * j + half], r2.at[source],
+            device_id=(across(j), x * 2 + half), device_id_type=MESH,
+        )
+
+    def codes_in(j, half):
+        return pltpu.make_async_remote_copy(
+            packed.at[half], arrived.at[2 * j + half], s2.at[2 * j + half], r2.at[2 * j + half],
+            device_id=(across(j), x * 2 + half), device_id_type=MESH,
+        )
+
+    def place(j, c):
+        return wbuf.at[j // 2, pl.ds(pl.multiple_of(64 * y1 + CHUNK * (2 * (j % 2) + c), 16), CHUNK), :]
+
+    def weight_copy(j, c):
+        return pltpu.make_async_remote_copy(
+            place(j, c), place(j, c), sf.at[j], rf.at[j], device_id=(sibling, t), device_id_type=MESH
         )
 
     def sum_out(k):
         peer = other(b, k)
         return pltpu.make_async_remote_copy(
-            pout.at[peer], pin.at[b], s3.at[k], r3.at[b], device_id=(group_of(ci, peer), t), device_id_type=MESH
+            pout.at[peer], pin.at[b], s3.at[k], r3.at[b], device_id=(member(peer), t), device_id_type=MESH
         )
 
     def sum_in(k):
         peer = other(b, k)
         return pltpu.make_async_remote_copy(
-            pout.at[b], pin.at[peer], s3.at[k], r3.at[peer], device_id=(group_of(ci, peer), t), device_id_type=MESH
-        )
-
-    for k in range(1, 8):
-        to_rank(k).start()
+            pout.at[b], pin.at[peer], s3.at[k], r3.at[peer], device_id=(member(peer), t), device_id_type=MESH
+        )
+
+    pl.semaphore_wait(barrier, 19)
+    for k in range(1, 4):
+        to_x(k).start()
     for k in range(1, 8):
         for half in range(2):
             hidden_out(k, half).start()
-    inbox[t] = msg[t]
+    inbox[x] = msg[x]
+
+    wbuf[:, pl.ds(pl.multiple_of(320 * (1 - y1), 64), 64), :] = jnp.zeros((2, 64, WIDE), BF16)
 
     loads[3].wait()
     swap = swap_matrix()
@@ -194,8 +219,8 @@
         sine = jnp.sin(angles)
         sinb[s * ROWS : (s + 1) * ROWS, :] = jnp.where(lane < HD // 2, -sine, sine)
 
+    loads[5].wait()
     loads[6].wait()
-    loads[7].wait()
     scale = 1.0 / math.sqrt(HD)
 
     def attend(r, carry):
@@ -211,22 +236,58 @@
 
     lax.fori_loop(0, EARLY, attend, 0)
 
-    loads[4].wait()
-    loads[5].wait()
-    for k in range(1, 8):
-        from_rank(k).wait_recv()
-    i = iota((CHUNK, 128), 0)
-    packed = i + 6 * lax.shift_right_logical(i * 205, 11)
-    pick = jnp.where(iota((CHUNK, 128), 1) == packed, 1.0, 0.0).astype(BF16)
-    got = dot(pick, inbox[...].reshape(128, WIDE + 128))
-    half_of = jnp.where(iota((128, WIDE), 1) >= HD, 1, 0)
-    spread = jnp.where(iota((128, WIDE), 0) == 2 * t + half_of, 1.0, 0.0).astype(BF16)
-    factor = dot(got[:, WIDE:].astype(BF16), spread)
-    place(ci)[...] = (basebuf[...].astype(F32) + got[:, :WIDE] * factor).astype(BF16)
-    for k in range(1, 8):
-        weight_copy(k, ci).start()
+    i = iota((40, 64), 0)
+    tens = lax.shift_right_logical(i * 205, 11)
+    pick = jnp.where(iota((40, 64), 1) == i + 6 * tens, 1.0, 0.0).astype(BF16)
+    i = iota((16, 128), 0)
+    column = 4 * x + jnp.where(i < 8, i, i - 6)
+    wanted = (iota((16, 128), 1) == column) & ((i < 2) | ((i >= 8) & (i < 10)))
+    choose = jnp.where(wanted, 1.0, 0.0).astype(BF16)
+    for k in range(1, 4):
+        from_x(k).wait_recv()
+    got = inbox[...].reshape(64, 2 * WIDE + 128)
+    factors = dot_t(choose, jnp.concatenate([got[:, 2 * WIDE :], jnp.zeros((64, 128), BF16)], axis=0))
+    body = dot(pick, got[:, : 2 * WIDE])
+    for half in range(2):
+        last = jnp.concatenate([factors[8 * half : 8 * half + 8, :], jnp.zeros((8, 128), F32)], axis=1)
+        whole = jnp.concatenate([body[:, half * WIDE : (half + 1) * WIDE], last], axis=0)
+        packed[half] = whole.astype(BF16)
+    for half in range(2):
+        for j in range(4):
+            codes_out(j, half).start()
 
     lax.fori_loop(EARLY, ROWS, attend, 0)
+
+    for load in base_loads:
+        load.wait()
+    i = iota((CHUNK, 96), 0)
+    tens = lax.shift_right_logical(i * 205, 11)
+    odd = lax.rem(tens, 2)
+    within = i - 10 * tens
+    pair = lax.div(tens, 2)
+    pick = jnp.where(iota((CHUNK, 96), 1) == odd * 48 + pair * 10 + within, 1.0, 0.0).astype(BF16)
+    i = iota((CHUNK, 256), 0)
+    tens = lax.shift_right_logical(i * 205, 11)
+    odd = lax.rem(tens, 2)
+    within = i - 10 * tens
+    pair = lax.div(tens, 2)
+    spread = jnp.where(iota((CHUNK, 256), 1) == odd * 128 + pair * 16 + within, 1.0, 0.0).astype(BF16)
+    for j in range(4):
+        for half in range(2):
+            codes_in(j, half).wait_recv()
+        both = arrived[2 * j : 2 * j + 2].reshape(96, WIDE)
+        update = dot(pick, both)
+        columns = []
+        for half in range(2):
+            ends = arrived[2 * j + half, 32:48, 0:128].astype(F32)
+            columns.append(
+                jnp.concatenate(
+                    [jnp.broadcast_to(ends[8 + part : 9 + part, :], (128, 128)) for part in range(2)], axis=0
+                )
+            )
+        factor = dot_t(spread, jnp.concatenate(columns, axis=1).astype(BF16))
+        place(j, core)[...] = (basebuf[j].astype(F32) + update * factor).astype(BF16)
+        weight_copy(j, core).start()
 
     for copy in own_hidden:
         copy.wait()
@@ -234,8 +295,9 @@
         for half in range(2):
             hidden_in(k, half).wait_recv()
     lefts = [hbuf[:, half].astype(F32).reshape(8 * FRESH, WINDOW).astype(BF16) for half in range(2)]
-    for k in range(1, 8):
-        weight_copy(k, other(ci, k)).wait_recv()
+    loads[4].wait()
+    for j in range(4):
+        weight_copy(j, 1 - core).wait_recv()
     partial = dot(lefts[0], wbuf[0]) + dot(lefts[1], wbuf[1])
     pout[...] = partial.reshape(8, FRESH, WIDE)
     for k in range(1, 8):
@@ -272,11 +334,15 @@
     result = jnp.concatenate([result[h * FRESH : (h + 1) * FRESH, :] for h in range(HEADS)], axis=1)
     out_ref[...] = result.reshape(STEPS, ROWS, HEADS * HD).astype(BF16)
 
-    for k in range(1, 8):
-        to_rank(k).wait_send()
+    for k in range(1, 4):
+        to_x(k).wait_send()
+    for j in range(4):
+        for half in range(2):
+            codes_out(j, half).wait_send()
+        weight_copy(j, core).wait_send()
+    for k in range(1, 8):
         for half in range(2):
             hidden_out(k, half).wait_send()
-        weight_copy(k, ci).wait_send()
         sum_out(k).wait_send()
 
 
@@ -292,12 +358,14 @@
             pltpu.VMEM((1, HD), F32),
             pltpu.VMEM((OWNED, 8 * WIDE), BF16),
             pltpu.VMEM((OWNED, 16), BF16),
-            pltpu.VMEM((CHUNK, WIDE), BF16),
+            pltpu.VMEM((4, CHUNK, WIDE), BF16),
             pltpu.VMEM((STEPS, ROWS, HEADS * HD), BF16),
             pltpu.VMEM((ROWS, CAP, HD), BF16),
             pltpu.VMEM((ROWS, CAP, HD), BF16),
-            pltpu.VMEM((8, 16, WIDE + 128), BF16),
-            pltpu.VMEM((8, 16, WIDE + 128), BF16),
+            pltpu.VMEM((4, 16, 2 * WIDE + 128), BF16),
+            pltpu.VMEM((4, 16, 2 * WIDE + 128), BF16),
+            pltpu.VMEM((2, 48, WIDE), BF16),
+            pltpu.VMEM((8, 48, WIDE), BF16),
             pltpu.VMEM((2, WINDOW, WIDE), BF16),
             pltpu.VMEM((8, 2, STEPS, ROWS, WINDOW), BF16),
             pltpu.VMEM((8, FRESH, WIDE), F32),
@@ -308,10 +376,11 @@
             pltpu.VMEM((ALLQ, HD), F32),
             pltpu.VMEM((FRESH, HD), F32),
             pltpu.VMEM((FRESH, HD), F32),
-            dma((8,)), dma((2,)),
-            dma((8,)), dma((8,)),
+            dma((7,)), dma((4,)), dma((2,)),
+            dma((4,)), dma((4,)),
             dma((8, 2)), dma((8, 2)),
             dma((8,)), dma((8,)),
+            dma((4,)), dma((4,)),
             dma((8,)), dma((8,)),
         ],
         compiler_params=pltpu.CompilerParams(

time: 40.4 us -> 40 us (0.990)
  the two profiles are of different devices: /device:TPU:49 before, /device:TPU:1 now
where the time goes in v2:
time: 40 us; the launch traced here: 39.8 us
  Pallas kernels  38.3 us (96%)
  local copies, waits for them, and re-layouts  1.42 us (4%)
    pallas_call x1, Pallas kernels, per_device(): pl.pallas_call(kernel, out_shape=jax.ShapeDtypeStruct((STEPS, ROWS, HEADS...  38.3 us
    unnamed x1, local copies, waits for them, and re-layouts  1.42 us

profile of v2, /device:TPU:1, one launch (start us, length us, event | category | flops | bytes accessed | tf_op | source)
XLA Modules:
  0.0 39.8 jit_solution(16979527220861590704)
XLA Ops:
  0.0 38.3 %project_and_attend.1 = bf16[3,8,1024]{2,1,0:T(8,128)(2,1)} custom-call(s32[8]{0:T(128)} %lengths_hbm.1, f32[1,128]{1,0:T(1,128)} %bitcast.1, bf16[10,2048]{1,0:T(8,128)(2,1)} %codes_hbm.1, bf16[10,16]{1,0:T(8,128)(2,1)} %scales_hbm.1, bf16[5120,256]{1,0:T(8,128)(2,1)} %base_hbm.1, bf16[3,8,5120]{2,1,0:T(8,128)(2,1)} %hidden_hbm.1, ...), custom_call_target="tpu_custom_call" | custom-call | tf_op jit(solution)/shard_map/project_and_attend/pallas_call | solution.py:351
  38.4 1.4 %copy.11 = bf16[3,8,1024]{2,1,0:T(8,128)(2,1)} copy(bf16[3,8,1024]{2,1,0:T(8,128)(2,1)} %project_and_attend.1) | data formatting | bytes 98304

commit v3 on v2

v3 whole, which is shorter than its diff:
```python
import functools
import math

import jax
import jax.numpy as jnp
from jax import lax
from jax.experimental import pallas as pl
from jax.experimental.pallas import tpu as pltpu
from jax.sharding import PartitionSpec as P

MESH = pl.DeviceIdType.MESH
F32 = jnp.float32
BF16 = jnp.bfloat16

STEPS = 3
ROWS = 8
HD = 128
HEADS = 8
CAP = 512
D = 5120
OWNED = 10
CHUNK = 80
WIDE = 256
SLICE = D // 8
FAR_FIRST = (4, 3, 5, 2, 6, 1, 7)
QROWS = STEPS * HEADS
ALLQ = ROWS * QROWS
FRESH = STEPS * ROWS
EARLY = 3


def iota(shape, dim):
    return lax.broadcasted_iota(jnp.int32, shape, dim)


def dot(a, b):
    return jnp.dot(a, b, preferred_element_type=F32)


def dot_t(a, b):
    return lax.dot_general(a, b, (((1,), (1,)), ((), ())), preferred_element_type=F32)


def swap_matrix():
    shape = (8, STEPS, 8, ALLQ)
    hit = iota(shape, 3) == iota(shape, 2) * QROWS + iota(shape, 1) * 8 + iota(shape, 0)
    return jnp.where(hit, 1.0, 0.0).astype(F32).reshape(ALLQ, ALLQ).astype(BF16)


def kernel(
    lengths_hbm, gain_hbm, codes_hbm, scales_hbm, base_hbm, hidden_hbm, queries_hbm, kc_hbm, vc_hbm,
    out_ref,
    lens, gain, basebuf, qbuf, hfull, kc, vc,
    boxc, boxs, inbox, packed, arrived, wbuf, hsend, hbuf, pout, pin, qall, acc, mbuf, lbuf, cosb, sinb,
    local_sem, base_sem, s1, r1, sh, rh, s2, r2, sf, rf, s3, r3,
):
    g = lax.axis_index("group")
    t = lax.axis_index("tp")
    core = lax.rem(g, 2)
    y = lax.rem(lax.div(g, 2), 8)
    zl = lax.div(g, 16)
    x, zh = lax.div(t, 2), lax.rem(t, 2)
    z = zh * 4 + zl

    def peer_x(k):
        return lax.rem(x + k, 4)

    def along_y(k):
        return zl * 16 + other(y, k) * 2 + core

    def along_z(k):
        there = other(z, k)
        return lax.rem(there, 4) * 16 + y * 2 + core, x * 2 + lax.div(there, 4)

    sibling = g + 1 - 2 * core

    def other(mine, k):
        return lax.rem(mine + k, 8)

    loads = [
        pltpu.make_async_copy(src, dst, local_sem.at[i])
        for i, (src, dst) in enumerate(
            [
                (hidden_hbm, hfull),
                (codes_hbm.at[:, pl.ds(pl.multiple_of(x * 2 * WIDE, 128), 2 * WIDE)], boxc.at[x]),
                (scales_hbm, boxs.at[x]),
                (lengths_hbm, lens),
                (queries_hbm, qbuf),
                (gain_hbm, gain),
                (kc_hbm, kc),
                (vc_hbm, vc),
            ]
        )
    ]
    hidden_load, code_load, scale_load, length_load, query_load, gain_load, key_load, value_load = loads
    base_loads = [
        pltpu.make_async_copy(
            base_hbm.at[pl.ds(pl.multiple_of((16 * j + 2 * y + core) * CHUNK, 16), CHUNK), :],
            basebuf.at[j],
            base_sem.at[j],
        )
        for j in range(4)
    ]

    barrier = pltpu.get_barrier_semaphore()
    hidden_load.start()
    for k in range(1, 4):
        pl.semaphore_signal(barrier, inc=1, device_id=(g, peer_x(k) * 2 + zh), device_id_type=MESH)
    for k in FAR_FIRST:
        pl.semaphore_signal(barrier, inc=1, device_id=along_z(k), device_id_type=MESH)
        pl.semaphore_signal(barrier, inc=1, device_id=(along_y(k), t), device_id_type=MESH)
    pl.semaphore_signal(barrier, inc=1, device_id=(sibling, t), device_id_type=MESH)
    for load in loads[1:] + base_loads:
        load.start()

    inbox[...] = jnp.zeros(inbox.shape, BF16)
    hidden_load.wait()
    everything = hfull[...].astype(F32).reshape(FRESH, D)
    for m in range(8):
        columns = [everything[:, j * 1280 + m * 160 : j * 1280 + m * 160 + 160] for j in range(4)]
        hsend[m] = jnp.concatenate(columns, axis=1).reshape(STEPS, ROWS, SLICE).astype(BF16)

    def to_x(k):
        peer = peer_x(k)
        device = (g, peer * 2 + zh)
        return (
            pltpu.make_async_remote_copy(
                codes_hbm.at[:, pl.ds(pl.multiple_of(peer * 2 * WIDE, 128), 2 * WIDE)], boxc.at[x],
                s1.at[k, 0], r1.at[x, 0], device_id=device, device_id_type=MESH,
            ),
            pltpu.make_async_remote_copy(
                scales_hbm, boxs.at[x], s1.at[k, 1], r1.at[x, 1], device_id=device, device_id_type=MESH
            ),
        )

    def from_x(k):
        peer = peer_x(k)
        device = (g, peer * 2 + zh)
        return (
            pltpu.make_async_remote_copy(
                codes_hbm.at[:, pl.ds(pl.multiple_of(x * 2 * WIDE, 128), 2 * WIDE)], boxc.at[peer],
                s1.at[k, 0], r1.at[peer, 0], device_id=device, device_id_type=MESH,
            ),
            pltpu.make_async_remote_copy(
                scales_hbm, boxs.at[peer], s1.at[k, 1], r1.at[peer, 1], device_id=device, device_id_type=MESH
            ),
        )

    def hidden_out(k):
        return pltpu.make_async_remote_copy(
            hsend.at[other(y, k)], hbuf.at[y], sh.at[k], rh.at[y], device_id=(along_y(k), t), device_id_type=MESH
        )

    def hidden_in(k):
        peer = other(y, k)
        return pltpu.make_async_remote_copy(
            hsend.at[y], hbuf.at[peer], sh.at[k], rh.at[peer], device_id=(along_y(k), t), device_id_type=MESH
        )

    def source(there):
        return lax.rem(there, 4) * 2 + lax.div(there, 4)

    def codes_out(k):
        return pltpu.make_async_remote_copy(
            packed.at[lax.div(other(z, k), 4)], arrived.at[source(z)], s2.at[k], r2.at[source(z)],
            device_id=along_z(k), device_id_type=MESH,
        )

    def codes_in(k):
        place_in = source(other(z, k))
        return pltpu.make_async_remote_copy(
            packed.at[zh], arrived.at[place_in], s2.at[k], r2.at[place_in],
            device_id=along_z(k), device_id_type=MESH,
        )

    def place(j, c):
        return wbuf.at[pl.ds(pl.multiple_of(CHUNK * (2 * j + c), 16), CHUNK), :]

    def weight_copy(j, c):
        return pltpu.make_async_remote_copy(
            place(j, c), place(j, c), sf.at[j], rf.at[j], device_id=(sibling, t), device_id_type=MESH
        )

    def sum_out(k):
        return pltpu.make_async_remote_copy(
            pout.at[other(y, k)], pin.at[y], s3.at[k], r3.at[y], device_id=(along_y(k), t), device_id_type=MESH
        )

    def sum_in(k):
        peer = other(y, k)
        return pltpu.make_async_remote_copy(
            pout.at[y], pin.at[peer], s3.at[k], r3.at[peer], device_id=(along_y(k), t), device_id_type=MESH
        )

    pl.semaphore_wait(barrier, 18)
    for k in (2, 1, 3):
        for copy in to_x(k):
            copy.start()
    for k in FAR_FIRST:
        hidden_out(k).start()
    hbuf[y] = hsend[y]

    query_load.wait()
    swap = swap_matrix()
    flat = qbuf[...].astype(F32).reshape(FRESH, HEADS * HD)
    stacked = jnp.concatenate([flat[:, h * HD : (h + 1) * HD] for h in range(HEADS)], axis=0)
    qall[...] = dot(swap, stacked.astype(BF16))

    length_load.wait()
    lane = iota((ROWS, HD), 1)
    row = iota((ROWS, HD), 0)
    start = jnp.zeros((ROWS, HD), F32)
    for r in range(ROWS):
        start = jnp.where(row == r, lens[r].astype(F32), start)
    ladder = jnp.where(lane < HD // 2, lane, lane - HD // 2).astype(F32)
    freqs = jnp.exp(-math.log(1000000.0) * ladder / (HD // 2))
    for s in range(STEPS):
        angles = (start + float(s)) * freqs
        cosb[s * ROWS : (s + 1) * ROWS, :] = jnp.cos(angles)
        sine = jnp.sin(angles)
        sinb[s * ROWS : (s + 1) * ROWS, :] = jnp.where(lane < HD // 2, -sine, sine)

    key_load.wait()
    value_load.wait()
    scale = 1.0 / math.sqrt(HD)

    def attend(r, carry):
        rows = pl.ds(pl.multiple_of(r * QROWS, 8), QROWS)
        scores = dot_t(qall[rows, :].astype(BF16), kc[r]) * scale
        scores = jnp.where(iota((QROWS, CAP), 1) < lens[r], scores, -1e30)
        highest = jnp.max(scores, axis=-1, keepdims=True)
        weights = jnp.exp(scores - highest)
        mbuf[rows, :] = jnp.broadcast_to(highest, (QROWS, HD))
        lbuf[rows, :] = jnp.broadcast_to(jnp.sum(weights, axis=-1, keepdims=True), (QROWS, HD))
        acc[rows, :] = dot(weights.astype(BF16), vc[r])
        return carry

    lax.fori_loop(0, EARLY, attend, 0)

    i = iota((40, 64), 0)
    tens = lax.shift_right_logical(i * 205, 11)
    pick = jnp.where(iota((40, 64), 1) == i + 6 * tens, 1.0, 0.0).astype(BF16)
    i = iota((16, 128), 0)
    column = 4 * x + jnp.where(i < 8, i, i - 6)
    wanted = (iota((16, 128), 1) == column) & ((i < 2) | ((i >= 8) & (i < 10)))
    choose = jnp.where(wanted, 1.0, 0.0).astype(BF16)
    code_load.wait()
    scale_load.wait()
    for k in range(1, 4):
        for copy in from_x(k):
            copy.wait_recv()
    for k in range(4):
        inbox[k, 0:OWNED, 0 : 2 * WIDE] = boxc[k]
        inbox[k, 0:OWNED, 2 * WIDE : 2 * WIDE + 16] = boxs[k]
    got = inbox[...].reshape(64, 2 * WIDE + 128)
    factors = dot_t(choose, jnp.concatenate([got[:, 2 * WIDE :], jnp.zeros((64, 128), BF16)], axis=0))
    body = dot(pick, got[:, : 2 * WIDE])
    for half in range(2):
        last = jnp.concatenate([factors[8 * half : 8 * half + 8, :], jnp.zeros((8, 128), F32)], axis=1)
        whole = jnp.concatenate([body[:, half * WIDE : (half + 1) * WIDE], last], axis=0)
        packed[half] = whole.astype(BF16)
    for k in FAR_FIRST:
        codes_out(k).start()
    arrived[source(z)] = packed[zh]

    lax.fori_loop(EARLY, ROWS, attend, 0)

    for load in base_loads:
        load.wait()
    i = iota((CHUNK, 96), 0)
    tens = lax.shift_right_logical(i * 205, 11)
    odd = lax.rem(tens, 2)
    within = i - 10 * tens
    pair = lax.div(tens, 2)
    pick = jnp.where(iota((CHUNK, 96), 1) == odd * 48 + pair * 10 + within, 1.0, 0.0).astype(BF16)
    i = iota((CHUNK, 256), 0)
    tens = lax.shift_right_logical(i * 205, 11)
    odd = lax.rem(tens, 2)
    within = i - 10 * tens
    pair = lax.div(tens, 2)
    spread = jnp.where(iota((CHUNK, 256), 1) == odd * 128 + pair * 16 + within, 1.0, 0.0).astype(BF16)
    for k in range(1, 8):
        codes_in(k).wait_recv()
    for j in range(4):
        both = arrived[2 * j : 2 * j + 2].reshape(96, WIDE)
        update = dot(pick, both)
        columns = []
        for half in range(2):
            ends = arrived[2 * j + half, 32:48, 0:128].astype(F32)
            columns.append(
                jnp.concatenate(
                    [jnp.broadcast_to(ends[8 + part : 9 + part, :], (128, 128)) for part in range(2)], axis=0
                )
            )
        factor = dot_t(spread, jnp.concatenate(columns, axis=1).astype(BF16))
        place(j, core)[...] = (basebuf[j].astype(F32) + update * factor).astype(BF16)
        weight_copy(j, core).start()

    for k in range(1, 8):
        hidden_in(k).wait_recv()
    left = hbuf[...].astype(F32).reshape(8 * FRESH, SLICE).astype(BF16)
    gain_load.wait()
    for j in range(4):
        weight_copy(j, 1 - core).wait_recv()
    partial = dot(left, wbuf[...])
    pout[...] = partial.reshape(8, FRESH, WIDE)
    for k in FAR_FIRST:
        sum_out(k).start()
    pin[y] = pout[y]
    swap = swap_matrix()
    everything = qall[...].astype(BF16)
    shape = (ROWS, STEPS, HEADS, FRESH)
    col = iota(shape, 3)
    slot = jnp.where(col >= 2 * ROWS, 2, jnp.where(col >= ROWS, 1, 0))
    seen = (col - slot * ROWS == iota(shape, 0)) & (slot <= iota(shape, 1))
    bias = jnp.where(seen, 0.0, -1e30).astype(F32).reshape(ALLQ, FRESH)
    for k in range(1, 8):
        sum_in(k).wait_recv()
    projected = pin[0]
    for m in range(1, 8):
        projected = projected + pin[m]

    keys = projected[:, :HD]
    meansq = jnp.mean(keys * keys, axis=-1, keepdims=True)
    keys = keys * lax.rsqrt(meansq + 1e-06) * gain[...]
    turned = jnp.concatenate([keys[:, HD // 2 :], keys[:, : HD // 2]], axis=1)
    keys = (keys * cosb[...] + turned * sinb[...]).astype(BF16)
    values = projected[:, HD:].astype(BF16)

    scores = dot_t(everything, keys) * scale + bias
    before = mbuf[...]
    highest = jnp.maximum(before[:, :1], jnp.max(scores, axis=-1, keepdims=True))
    weights = jnp.exp(scores - highest)
    shrink = jnp.exp(before - highest)
    total = shrink * lbuf[...] + jnp.sum(weights, axis=-1, keepdims=True)
    result = (shrink * acc[...] + dot(weights.astype(BF16), values)) / total
    result = dot(swap, result.astype(BF16))
    result = jnp.concatenate([result[h * FRESH : (h + 1) * FRESH, :] for h in range(HEADS)], axis=1)
    out_ref[...] = result.reshape(STEPS, ROWS, HEADS * HD).astype(BF16)

    for k in range(1, 4):
        for copy in to_x(k):
            copy.wait_send()
    for j in range(4):
        weight_copy(j, core).wait_send()
    for k in range(1, 8):
        codes_out(k).wait_send()
        hidden_out(k).wait_send()
        sum_out(k).wait_send()


def per_device(hidden, queries, key_cache, value_cache, lengths, key_gain, base_weight, delta_codes, delta_scales):
    dma = pltpu.SemaphoreType.DMA
    return pl.pallas_call(
        kernel,
        out_shape=jax.ShapeDtypeStruct((STEPS, ROWS, HEADS * HD), BF16),
        in_specs=[pl.BlockSpec(memory_space=pl.ANY)] * 9,
        out_specs=pl.BlockSpec(memory_space=pltpu.VMEM),
        scratch_shapes=[
            pltpu.SMEM((ROWS,), jnp.int32),
            pltpu.VMEM((1, HD), F32),
            pltpu.VMEM((4, CHUNK, WIDE), BF16),
            pltpu.VMEM((STEPS, ROWS, HEADS * HD), BF16),
            pltpu.VMEM((STEPS, ROWS, D), BF16),
            pltpu.VMEM((ROWS, CAP, HD), BF16),
            pltpu.VMEM((ROWS, CAP, HD), BF16),
            pltpu.VMEM((4, OWNED, 2 * WIDE), BF16),
            pltpu.VMEM((4, OWNED, 16), BF16),
            pltpu.VMEM((4, 16, 2 * WIDE + 128), BF16),
            pltpu.VMEM((2, 48, WIDE), BF16),
            pltpu.VMEM((8, 48, WIDE), BF16),
            pltpu.VMEM((SLICE, WIDE), BF16),
            pltpu.VMEM((8, STEPS, ROWS, SLICE), BF16),
            pltpu.VMEM((8, STEPS, ROWS, SLICE), BF16),
            pltpu.VMEM((8, FRESH, WIDE), F32),
            pltpu.VMEM((8, FRESH, WIDE), F32),
            pltpu.VMEM((ALLQ, HD), F32),
            pltpu.VMEM((ALLQ, HD), F32),
            pltpu.VMEM((ALLQ, HD), F32),
            pltpu.VMEM((ALLQ, HD), F32),
            pltpu.VMEM((FRESH, HD), F32),
            pltpu.VMEM((FRESH, HD), F32),
            dma((8,)), dma((4,)),
            dma((4, 2)), dma((4, 2)),
            dma((8,)), dma((8,)),
            dma((8,)), dma((8,)),
            dma((4,)), dma((4,)),
            dma((8,)), dma((8,)),
        ],
        compiler_params=pltpu.CompilerParams(
            collective_id=0, has_side_effects=True, vmem_limit_bytes=56 * 1024 * 1024
        ),
        name="project_and_attend",
    )(
        lengths, key_gain.reshape(1, HD), delta_codes, delta_scales, base_weight, hidden, queries, key_cache, value_cache,
    )


def solution(mesh):
    return jax.shard_map(
        per_device,
        mesh=mesh,
        in_specs=(
            P(None, "group", None),
            P(None, "group", "tp"),
            P("group", None, "tp"),
            P("group", None, "tp"),
            P("group"),
            P(),
            P(None, "tp"),
            P(("group", "tp"), None),
            P(("group", "tp"), None),
        ),
        out_specs=P(None, "group", "tp"),
        check_vma=False,
    )
```

time: 40 us -> 36.8 us (0.920)
  Pallas kernels: 38.3 us -> 35.2 us
    pallas_call x1, Pallas kernels: 38.3 us -> 35.2 us  [per_device(): pl.pallas_call(kernel, out_shape=jax.ShapeDtypeStruct((STEPS, ROWS, HEADS...]
where the time goes in v3:
time: 36.8 us; the launch traced here: 36.7 us
  Pallas kernels  35.2 us (96%)
  local copies, waits for them, and re-layouts  1.42 us (4%)
    pallas_call x1, Pallas kernels, per_device(): pl.pallas_call(kernel, out_shape=jax.ShapeDtypeStruct((STEPS, ROWS, HEADS...  35.2 us
    unnamed x1, local copies, waits for them, and re-layouts  1.42 us

profile of v3, /device:TPU:1, one launch (start us, length us, event | category | flops | bytes accessed | tf_op | source)
XLA Modules:
  0.0 36.7 jit_solution(8191416599431845778)
XLA Ops:
  0.0 35.2 %project_and_attend.1 = bf16[3,8,1024]{2,1,0:T(8,128)(2,1)} custom-call(s32[8]{0:T(128)} %lengths_hbm.1, f32[1,128]{1,0:T(1,128)} %bitcast.1, bf16[10,2048]{1,0:T(8,128)(2,1)} %codes_hbm.1, bf16[10,16]{1,0:T(8,128)(2,1)} %scales_hbm.1, bf16[5120,256]{1,0:T(8,128)(2,1)} %base_hbm.1, bf16[3,8,5120]{2,1,0:T(8,128)(2,1)} %hidden_hbm.1, ...), custom_call_target="tpu_custom_call" | custom-call | tf_op jit(solution)/shard_map/project_and_attend/pallas_call | solution.py:354
  35.2 1.4 %copy.11 = bf16[3,8,1024]{2,1,0:T(8,128)(2,1)} copy(bf16[3,8,1024]{2,1,0:T(8,128)(2,1)} %project_and_attend.1) | data formatting | bytes 98304

commit v4 on v3

--- a/solution.py
+++ b/solution.py
@@ -51,7 +51,7 @@
     lengths_hbm, gain_hbm, codes_hbm, scales_hbm, base_hbm, hidden_hbm, queries_hbm, kc_hbm, vc_hbm,
     out_ref,
     lens, gain, basebuf, qbuf, hfull, kc, vc,
-    boxc, boxs, inbox, packed, arrived, wbuf, hsend, hbuf, pout, pin, qall, acc, mbuf, lbuf, cosb, sinb,
+    boxc, boxs, inbox, packed, arrived, wbuf, hsend, hbuf, left, pout, pin, qflat, qall, acc, mbuf, lbuf, cosb, sinb,
     local_sem, base_sem, s1, r1, sh, rh, s2, r2, sf, rf, s3, r3,
 ):
     g = lax.axis_index("group")
@@ -108,6 +108,7 @@
         pl.semaphore_signal(barrier, inc=1, device_id=(g, peer_x(k) * 2 + zh), device_id_type=MESH)
     for k in FAR_FIRST:
         pl.semaphore_signal(barrier, inc=1, device_id=along_z(k), device_id_type=MESH)
+    for k in FAR_FIRST:
         pl.semaphore_signal(barrier, inc=1, device_id=(along_y(k), t), device_id_type=MESH)
     pl.semaphore_signal(barrier, inc=1, device_id=(sibling, t), device_id_type=MESH)
     for load in loads[1:] + base_loads:
@@ -117,8 +118,10 @@
     hidden_load.wait()
     everything = hfull[...].astype(F32).reshape(FRESH, D)
     for m in range(8):
-        columns = [everything[:, j * 1280 + m * 160 : j * 1280 + m * 160 + 160] for j in range(4)]
-        hsend[m] = jnp.concatenate(columns, axis=1).reshape(STEPS, ROWS, SLICE).astype(BF16)
+        for c in range(2):
+            starts = [(16 * j + 2 * m + c) * CHUNK for j in range(4)]
+            columns = jnp.concatenate([everything[:, a : a + CHUNK] for a in starts], axis=1)
+            hsend[m, c] = columns.reshape(STEPS, ROWS, SLICE // 2).astype(BF16)
 
     def to_x(k):
         peer = peer_x(k)
@@ -173,12 +176,9 @@
             device_id=along_z(k), device_id_type=MESH,
         )
 
-    def place(j, c):
-        return wbuf.at[pl.ds(pl.multiple_of(CHUNK * (2 * j + c), 16), CHUNK), :]
-
-    def weight_copy(j, c):
-        return pltpu.make_async_remote_copy(
-            place(j, c), place(j, c), sf.at[j], rf.at[j], device_id=(sibling, t), device_id_type=MESH
+    def weight_copy(c):
+        return pltpu.make_async_remote_copy(
+            wbuf.at[c], wbuf.at[c], sf, rf, device_id=(sibling, t), device_id_type=MESH
         )
 
     def sum_out(k):
@@ -204,6 +204,7 @@
     swap = swap_matrix()
     flat = qbuf[...].astype(F32).reshape(FRESH, HEADS * HD)
     stacked = jnp.concatenate([flat[:, h * HD : (h + 1) * HD] for h in range(HEADS)], axis=0)
+    qflat[...] = stacked.astype(BF16)
     qall[...] = dot(swap, stacked.astype(BF16))
 
     length_load.wait()
@@ -230,9 +231,14 @@
         scores = jnp.where(iota((QROWS, CAP), 1) < lens[r], scores, -1e30)
         highest = jnp.max(scores, axis=-1, keepdims=True)
         weights = jnp.exp(scores - highest)
-        mbuf[rows, :] = jnp.broadcast_to(highest, (QROWS, HD))
-        lbuf[rows, :] = jnp.broadcast_to(jnp.sum(weights, axis=-1, keepdims=True), (QROWS, HD))
-        acc[rows, :] = dot(weights.astype(BF16), vc[r])
+        total = jnp.sum(weights, axis=-1, keepdims=True)
+        mixed = dot(weights.astype(BF16), vc[r])
+        for s in range(STEPS):
+            there = pl.ds(s * ROWS + r, HEADS, stride=FRESH)
+            these = slice(s * HEADS, (s + 1) * HEADS)
+            mbuf[there, :] = jnp.broadcast_to(highest[these, :], (HEADS, HD))
+            lbuf[there, :] = jnp.broadcast_to(total[these, :], (HEADS, HD))
+            acc[there, :] = mixed[these, :]
         return carry
 
     lax.fori_loop(0, EARLY, attend, 0)
@@ -280,10 +286,15 @@
     pair = lax.div(tens, 2)
     spread = jnp.where(iota((CHUNK, 256), 1) == odd * 128 + pair * 16 + within, 1.0, 0.0).astype(BF16)
     for k in range(1, 8):
+        hidden_in(k).wait_recv()
+    for c in range(2):
+        left[c] = hbuf[:, c].astype(F32).reshape(8 * FRESH, SLICE // 2).astype(BF16)
+    gain_load.wait()
+    for k in range(1, 8):
         codes_in(k).wait_recv()
+    sides, factors = [], []
     for j in range(4):
-        both = arrived[2 * j : 2 * j + 2].reshape(96, WIDE)
-        update = dot(pick, both)
+        sides.append(arrived[2 * j : 2 * j + 2].reshape(96, WIDE))
         columns = []
         for half in range(2):
             ends = arrived[2 * j + half, 32:48, 0:128].astype(F32)
@@ -292,28 +303,36 @@
                     [jnp.broadcast_to(ends[8 + part : 9 + part, :], (128, 128)) for part in range(2)], axis=0
                 )
             )
-        factor = dot_t(spread, jnp.concatenate(columns, axis=1).astype(BF16))
-        place(j, core)[...] = (basebuf[j].astype(F32) + update * factor).astype(BF16)
-        weight_copy(j, core).start()
-
-    for k in range(1, 8):
-        hidden_in(k).wait_recv()
-    left = hbuf[...].astype(F32).reshape(8 * FRESH, SLICE).astype(BF16)
-    gain_load.wait()
+        factors.append(jnp.concatenate(columns, axis=1).astype(BF16))
+    update = dot(pick, jnp.concatenate(sides, axis=1))
+    factor = dot_t(spread, jnp.concatenate(factors, axis=0))
     for j in range(4):
-        weight_copy(j, 1 - core).wait_recv()
-    partial = dot(left, wbuf[...])
+        part = slice(j * WIDE, (j + 1) * WIDE)
+        wbuf[core, j * CHUNK : (j + 1) * CHUNK, :] = (
+            basebuf[j].astype(F32) + update[:, part] * factor[:, part]
+        ).astype(BF16)
+    weight_copy(core).start()
+
+    partial = dot(left[core], wbuf[core])
+    weight_copy(1 - core).wait_recv()
+    partial = partial + dot(left[1 - core], wbuf[1 - core])
     pout[...] = partial.reshape(8, FRESH, WIDE)
     for k in FAR_FIRST:
         sum_out(k).start()
     pin[y] = pout[y]
-    swap = swap_matrix()
-    everything = qall[...].astype(BF16)
-    shape = (ROWS, STEPS, HEADS, FRESH)
+    everything = qflat[...]
+    shape = (HEADS, STEPS, ROWS, FRESH)
     col = iota(shape, 3)
     slot = jnp.where(col >= 2 * ROWS, 2, jnp.where(col >= ROWS, 1, 0))
-    seen = (col - slot * ROWS == iota(shape, 0)) & (slot <= iota(shape, 1))
+    seen = (col - slot * ROWS == iota(shape, 2)) & (slot <= iota(shape, 1))
     bias = jnp.where(seen, 0.0, -1e30).astype(F32).reshape(ALLQ, FRESH)
+    for k in range(1, 4):
+        for copy in to_x(k):
+            copy.wait_send()
+    for k in FAR_FIRST:
+        hidden_out(k).wait_send()
+        codes_out(k).wait_send()
+    weight_copy(core).wait_send()
     for k in range(1, 8):
         sum_in(k).wait_recv()
     projected = pin[0]
@@ -334,18 +353,10 @@
     shrink = jnp.exp(before - highest)
     total = shrink * lbuf[...] + jnp.sum(weights, axis=-1, keepdims=True)
     result = (shrink * acc[...] + dot(weights.astype(BF16), values)) / total
-    result = dot(swap, result.astype(BF16))
     result = jnp.concatenate([result[h * FRESH : (h + 1) * FRESH, :] for h in range(HEADS)], axis=1)
     out_ref[...] = result.reshape(STEPS, ROWS, HEADS * HD).astype(BF16)
 
-    for k in range(1, 4):
-        for copy in to_x(k):
-            copy.wait_send()
-    for j in range(4):
-        weight_copy(j, core).wait_send()
-    for k in range(1, 8):
-        codes_out(k).wait_send()
-        hidden_out(k).wait_send()
+    for k in FAR_FIRST:
         sum_out(k).wait_send()
 
 
@@ -353,7 +364,7 @@
     dma = pltpu.SemaphoreType.DMA
     return pl.pallas_call(
         kernel,
-        out_shape=jax.ShapeDtypeStruct((STEPS, ROWS, HEADS * HD), BF16),
+        out_shape=pltpu.VMEM((STEPS, ROWS, HEADS * HD), BF16),
         in_specs=[pl.BlockSpec(memory_space=pl.ANY)] * 9,
         out_specs=pl.BlockSpec(memory_space=pltpu.VMEM),
         scratch_shapes=[
@@ -369,11 +380,13 @@
             pltpu.VMEM((4, 16, 2 * WIDE + 128), BF16),
             pltpu.VMEM((2, 48, WIDE), BF16),
             pltpu.VMEM((8, 48, WIDE), BF16),
-            pltpu.VMEM((SLICE, WIDE), BF16),
-            pltpu.VMEM((8, STEPS, ROWS, SLICE), BF16),
-            pltpu.VMEM((8, STEPS, ROWS, SLICE), BF16),
+            pltpu.VMEM((2, SLICE // 2, WIDE), BF16),
+            pltpu.VMEM((8, 2, STEPS, ROWS, SLICE // 2), BF16),
+            pltpu.VMEM((8, 2, STEPS, ROWS, SLICE // 2), BF16),
+            pltpu.VMEM((2, 8 * FRESH, SLICE // 2), BF16),
             pltpu.VMEM((8, FRESH, WIDE), F32),
             pltpu.VMEM((8, FRESH, WIDE), F32),
+            pltpu.VMEM((ALLQ, HD), BF16),
             pltpu.VMEM((ALLQ, HD), F32),
             pltpu.VMEM((ALLQ, HD), F32),
             pltpu.VMEM((ALLQ, HD), F32),
@@ -384,7 +397,7 @@
             dma((4, 2)), dma((4, 2)),
             dma((8,)), dma((8,)),
             dma((8,)), dma((8,)),
-            dma((4,)), dma((4,)),
+            dma, dma,
             dma((8,)), dma((8,)),
         ],
         compiler_params=pltpu.CompilerParams(

time: 36.8 us -> 34.7 us (0.943)
  Pallas kernels: 35.2 us -> 34 us
  local copies, waits for them, and re-layouts: 1.42 us -> 0.62 us
    pallas_call x1, Pallas kernels: 35.2 us -> 34 us  [per_device(): pl.pallas_call(kernel, out_shape=pltpu.VMEM((STEPS, ROWS, HEADS * HD), BF...]
    unnamed x1, local copies, waits for them, and re-layouts: 1.42 us -> 0.62 us
where the time goes in v4:
time: 34.7 us; the launch traced here: 34.6 us
  Pallas kernels  34 us (98%)
  local copies, waits for them, and re-layouts  0.62 us (2%)
    pallas_call x1, Pallas kernels, per_device(): pl.pallas_call(kernel, out_shape=pltpu.VMEM((STEPS, ROWS, HEADS * HD), BF...  34 us

profile of v4, /device:TPU:1, one launch (start us, length us, event | category | flops | bytes accessed | tf_op | source)
XLA Modules:
  0.0 34.6 jit_solution(5498573154015256319)
XLA Ops:
  0.0 34.0 %project_and_attend.1 = bf16[3,8,1024]{2,1,0:T(8,128)(2,1)S(1)} custom-call(s32[8]{0:T(128)} %lengths_hbm.1, f32[1,128]{1,0:T(1,128)} %bitcast.1, bf16[10,2048]{1,0:T(8,128)(2,1)} %codes_hbm.1, bf16[10,16]{1,0:T(8,128)(2,1)} %scales_hbm.1, bf16[5120,256]{1,0:T(8,128)(2,1)} %base_hbm.1, bf16[3,8,5120]{2,1,0:T(8,128)(2,1)} %hidden_hbm.1, ...), custom_call_target="tpu_custom_call" | custom-call | tf_op jit(solution)/shard_map/project_and_attend/pallas_call | solution.py:365
  34.0 0.6 %copy.11 = bf16[3,8,1024]{2,1,0:T(8,128)(2,1)} copy(bf16[3,8,1024]{2,1,0:T(8,128)(2,1)S(1)} %project_and_attend.1) | data formatting | bytes 98304

commit v5 on v4

--- a/solution.py
+++ b/solution.py
@@ -23,10 +23,11 @@
 WIDE = 256
 SLICE = D // 8
 FAR_FIRST = (4, 3, 5, 2, 6, 1, 7)
+Y_ORDER = (0, 1, 2, 3, 7, 6, 5, 4)
 QROWS = STEPS * HEADS
 ALLQ = ROWS * QROWS
 FRESH = STEPS * ROWS
-EARLY = 3
+EARLY = 0
 
 
 def iota(shape, dim):
@@ -52,7 +53,7 @@
     out_ref,
     lens, gain, basebuf, qbuf, hfull, kc, vc,
     boxc, boxs, inbox, packed, arrived, wbuf, hsend, hbuf, left, pout, pin, qflat, qall, acc, mbuf, lbuf, cosb, sinb,
-    local_sem, base_sem, s1, r1, sh, rh, s2, r2, sf, rf, s3, r3,
+    local_sem, base_sem, s1, r1, sh, rh, s2, r2, sf, rf, s3, r3, ready_y, ready_z,
 ):
     g = lax.axis_index("group")
     t = lax.axis_index("tp")
@@ -102,27 +103,6 @@
         for j in range(4)
     ]
 
-    barrier = pltpu.get_barrier_semaphore()
-    hidden_load.start()
-    for k in range(1, 4):
-        pl.semaphore_signal(barrier, inc=1, device_id=(g, peer_x(k) * 2 + zh), device_id_type=MESH)
-    for k in FAR_FIRST:
-        pl.semaphore_signal(barrier, inc=1, device_id=along_z(k), device_id_type=MESH)
-    for k in FAR_FIRST:
-        pl.semaphore_signal(barrier, inc=1, device_id=(along_y(k), t), device_id_type=MESH)
-    pl.semaphore_signal(barrier, inc=1, device_id=(sibling, t), device_id_type=MESH)
-    for load in loads[1:] + base_loads:
-        load.start()
-
-    inbox[...] = jnp.zeros(inbox.shape, BF16)
-    hidden_load.wait()
-    everything = hfull[...].astype(F32).reshape(FRESH, D)
-    for m in range(8):
-        for c in range(2):
-            starts = [(16 * j + 2 * m + c) * CHUNK for j in range(4)]
-            columns = jnp.concatenate([everything[:, a : a + CHUNK] for a in starts], axis=1)
-            hsend[m, c] = columns.reshape(STEPS, ROWS, SLICE // 2).astype(BF16)
-
     def to_x(k):
         peer = peer_x(k)
         device = (g, peer * 2 + zh)
@@ -192,14 +172,60 @@
             pout.at[y], pin.at[peer], s3.at[k], r3.at[peer], device_id=(along_y(k), t), device_id_type=MESH
         )
 
-    pl.semaphore_wait(barrier, 18)
+    barrier = pltpu.get_barrier_semaphore()
+    half_y = lax.div(y, 4)
+    rank = y + half_y * (11 - 2 * y)
+    y_devices = [(zl * 16 + there * 2 + core, t) for there in Y_ORDER]
+    z_devices = [((there % 4) * 16 + y * 2 + core, x * 2 + there // 4) for there in range(8)]
+
+    for k in (2, 1, 3):
+        pl.semaphore_signal(barrier, inc=1, device_id=(g, peer_x(k) * 2 + zh), device_id_type=MESH)
+    pl.semaphore_signal(barrier, inc=1, device_id=(sibling, t), device_id_type=MESH)
+    hidden_load.start()
+    for n in range(1, 8):
+
+        @pl.when(z < n)
+        def _(n=n):
+            pl.semaphore_signal(barrier, inc=1, device_id=z_devices[n], device_id_type=MESH)
+
+        @pl.when(rank < n)
+        def _(n=n):
+            pl.semaphore_signal(barrier, inc=1, device_id=y_devices[n], device_id_type=MESH)
+
+    pl.semaphore_wait(barrier, 4 + z + rank)
     for k in (2, 1, 3):
         for copy in to_x(k):
             copy.start()
+    for n in range(7):
+
+        @pl.when(z > n)
+        def _(n=n):
+            pl.semaphore_signal(ready_z, inc=1, device_id=z_devices[n], device_id_type=MESH)
+
+        @pl.when(rank > n)
+        def _(n=n):
+            pl.semaphore_signal(ready_y, inc=1, device_id=y_devices[n], device_id_type=MESH)
+
+    for load in loads[1:] + base_loads:
+        load.start()
+    inbox[...] = jnp.zeros(inbox.shape, BF16)
+
+    hidden_load.wait()
+    everything = hfull[...].astype(F32).reshape(FRESH, D)
+    for m in range(8):
+        for c in range(2):
+            starts = [(16 * j + 2 * m + c) * CHUNK for j in range(4)]
+            columns = jnp.concatenate([everything[:, a : a + CHUNK] for a in starts], axis=1)
+            hsend[m, c] = columns.reshape(STEPS, ROWS, SLICE // 2).astype(BF16)
+
+    hbuf[y] = hsend[y]
+
+    @pl.when(rank < 7)
+    def _():
+        pl.semaphore_wait(ready_y, 7 - rank)
+
     for k in FAR_FIRST:
         hidden_out(k).start()
-    hbuf[y] = hsend[y]
-
     query_load.wait()
     swap = swap_matrix()
     flat = qbuf[...].astype(F32).reshape(FRESH, HEADS * HD)
@@ -242,6 +268,7 @@
         return carry
 
     lax.fori_loop(0, EARLY, attend, 0)
+
 
     i = iota((40, 64), 0)
     tens = lax.shift_right_logical(i * 205, 11)
@@ -265,6 +292,10 @@
         last = jnp.concatenate([factors[8 * half : 8 * half + 8, :], jnp.zeros((8, 128), F32)], axis=1)
         whole = jnp.concatenate([body[:, half * WIDE : (half + 1) * WIDE], last], axis=0)
         packed[half] = whole.astype(BF16)
+    @pl.when(z < 7)
+    def _():
+        pl.semaphore_wait(ready_z, 7 - z)
+
     for k in FAR_FIRST:
         codes_out(k).start()
     arrived[source(z)] = packed[zh]
@@ -399,6 +430,7 @@
             dma((8,)), dma((8,)),
             dma, dma,
             dma((8,)), dma((8,)),
+            pltpu.SemaphoreType.REGULAR, pltpu.SemaphoreType.REGULAR,
         ],
         compiler_params=pltpu.CompilerParams(
             collective_id=0, has_side_effects=True, vmem_limit_bytes=56 * 1024 * 1024

time: 34.7 us -> 34.5 us (level)
  no operation moved by 1% of the time
where the time goes in v5:
time: 34.5 us; the launch traced here: 34.3 us
  Pallas kernels  33.7 us (98%)
  local copies, waits for them, and re-layouts  0.62 us (2%)
    pallas_call x1, Pallas kernels, per_device(): pl.pallas_call(kernel, out_shape=pltpu.VMEM((STEPS, ROWS, HEADS * HD), BF...  33.7 us

profile of v5, /device:TPU:1, one launch (start us, length us, event | category | flops | bytes accessed | tf_op | source)
XLA Modules:
  0.0 34.3 jit_solution(15338252020008646552)
XLA Ops:
  0.0 33.7 %project_and_attend.1 = bf16[3,8,1024]{2,1,0:T(8,128)(2,1)S(1)} custom-call(s32[8]{0:T(128)} %lengths_hbm.1, f32[1,128]{1,0:T(1,128)} %bitcast.1, bf16[10,2048]{1,0:T(8,128)(2,1)} %codes_hbm.1, bf16[10,16]{1,0:T(8,128)(2,1)} %scales_hbm.1, bf16[5120,256]{1,0:T(8,128)(2,1)} %base_hbm.1, bf16[3,8,5120]{2,1,0:T(8,128)(2,1)} %hidden_hbm.1, ...), custom_call_target="tpu_custom_call" | custom-call | tf_op jit(solution)/shard_map/project_and_attend/pallas_call | solution.py:396
  33.7 0.6 %copy.11 = bf16[3,8,1024]{2,1,0:T(8,128)(2,1)} copy(bf16[3,8,1024]{2,1,0:T(8,128)(2,1)S(1)} %project_and_attend.1) | data formatting | bytes 98304

commit v6 on v5

--- a/solution.py
+++ b/solution.py
@@ -53,7 +53,7 @@
     out_ref,
     lens, gain, basebuf, qbuf, hfull, kc, vc,
     boxc, boxs, inbox, packed, arrived, wbuf, hsend, hbuf, left, pout, pin, qflat, qall, acc, mbuf, lbuf, cosb, sinb,
-    local_sem, base_sem, s1, r1, sh, rh, s2, r2, sf, rf, s3, r3, ready_y, ready_z,
+    local_sem, base_sem, s1, r1, sh, rh, s2, r2, sf, rf, s3, r3, ready_y, ready_z, ready_far,
 ):
     g = lax.axis_index("group")
     t = lax.axis_index("tp")
@@ -143,10 +143,10 @@
     def source(there):
         return lax.rem(there, 4) * 2 + lax.div(there, 4)
 
-    def codes_out(k):
-        return pltpu.make_async_remote_copy(
-            packed.at[lax.div(other(z, k), 4)], arrived.at[source(z)], s2.at[k], r2.at[source(z)],
-            device_id=along_z(k), device_id_type=MESH,
+    def codes_out(n):
+        return pltpu.make_async_remote_copy(
+            packed.at[n // 4], arrived.at[source(z)], s2.at[n], r2.at[source(z)],
+            device_id=z_devices[n], device_id_type=MESH,
         )
 
     def codes_in(k):
@@ -198,9 +198,15 @@
             copy.start()
     for n in range(7):
 
-        @pl.when(z > n)
+        @pl.when((z > n) & (zh == n // 4))
         def _(n=n):
             pl.semaphore_signal(ready_z, inc=1, device_id=z_devices[n], device_id_type=MESH)
+
+        if n < 4:
+
+            @pl.when(zh == 1)
+            def _(n=n):
+                pl.semaphore_signal(ready_far, inc=1, device_id=z_devices[n], device_id_type=MESH)
 
         @pl.when(rank > n)
         def _(n=n):
@@ -292,12 +298,27 @@
         last = jnp.concatenate([factors[8 * half : 8 * half + 8, :], jnp.zeros((8, 128), F32)], axis=1)
         whole = jnp.concatenate([body[:, half * WIDE : (half + 1) * WIDE], last], axis=0)
         packed[half] = whole.astype(BF16)
-    @pl.when(z < 7)
+    @pl.when(zh == 1)
     def _():
-        pl.semaphore_wait(ready_z, 7 - z)
-
-    for k in FAR_FIRST:
-        codes_out(k).start()
+        for n in range(4):
+            codes_out(n).start()
+
+    @pl.when(zl < 3)
+    def _():
+        pl.semaphore_wait(ready_z, 3 - zl)
+
+    for n in range(8):
+
+        @pl.when((z != n) & (zh == n // 4))
+        def _(n=n):
+            codes_out(n).start()
+
+    @pl.when(zh == 0)
+    def _():
+        pl.semaphore_wait(ready_far, 4)
+        for n in range(4, 8):
+            codes_out(n).start()
+
     arrived[source(z)] = packed[zh]
 
     lax.fori_loop(EARLY, ROWS, attend, 0)
@@ -362,7 +383,12 @@
             copy.wait_send()
     for k in FAR_FIRST:
         hidden_out(k).wait_send()
-        codes_out(k).wait_send()
+    for n in range(8):
+
+        @pl.when(z != n)
+        def _(n=n):
+            codes_out(n).wait_send()
+
     weight_copy(core).wait_send()
     for k in range(1, 8):
         sum_in(k).wait_recv()
@@ -430,7 +456,7 @@
             dma((8,)), dma((8,)),
             dma, dma,
             dma((8,)), dma((8,)),
-            pltpu.SemaphoreType.REGULAR, pltpu.SemaphoreType.REGULAR,
+            pltpu.SemaphoreType.REGULAR, pltpu.SemaphoreType.REGULAR, pltpu.SemaphoreType.REGULAR,
         ],
         compiler_params=pltpu.CompilerParams(
             collective_id=0, has_side_effects=True, vmem_limit_bytes=56 * 1024 * 1024

time: 34.5 us -> 33.7 us (0.977)
  Pallas kernels: 33.7 us -> 32.9 us
    pallas_call x1, Pallas kernels: 33.7 us -> 32.9 us  [per_device(): pl.pallas_call(kernel, out_shape=pltpu.VMEM((STEPS, ROWS, HEADS * HD), BF...]
where the time goes in v6:
time: 33.7 us; the launch traced here: 33.6 us
  Pallas kernels  32.9 us (98%)
  local copies, waits for them, and re-layouts  0.62 us (2%)
    pallas_call x1, Pallas kernels, per_device(): pl.pallas_call(kernel, out_shape=pltpu.VMEM((STEPS, ROWS, HEADS * HD), BF...  32.9 us

profile of v6, /device:TPU:1, one launch (start us, length us, event | category | flops | bytes accessed | tf_op | source)
XLA Modules:
  0.0 33.6 jit_solution(2095509492072699199)
XLA Ops:
  0.0 32.9 %project_and_attend.1 = bf16[3,8,1024]{2,1,0:T(8,128)(2,1)S(1)} custom-call(s32[8]{0:T(128)} %lengths_hbm.1, f32[1,128]{1,0:T(1,128)} %bitcast.1, bf16[10,2048]{1,0:T(8,128)(2,1)} %codes_hbm.1, bf16[10,16]{1,0:T(8,128)(2,1)} %scales_hbm.1, bf16[5120,256]{1,0:T(8,128)(2,1)} %base_hbm.1, bf16[3,8,5120]{2,1,0:T(8,128)(2,1)} %hidden_hbm.1, ...), custom_call_target="tpu_custom_call" | custom-call | tf_op jit(solution)/shard_map/project_and_attend/pallas_call | solution.py:422
  33.0 0.6 %copy.11 = bf16[3,8,1024]{2,1,0:T(8,128)(2,1)} copy(bf16[3,8,1024]{2,1,0:T(8,128)(2,1)S(1)} %project_and_attend.1) | data formatting | bytes 98304
